TPU v7x, 32 devices: a whole 2x2x4 slice. The times are simulated.
32 devices in a mesh: dp: 4 (over z), row: 4 (over x, core), col: 2 (over y).
Axes of the slice: x: 2, y: 2, z: 4, core: 2. Of those that a mesh axis runs over, the one named last changes fastest.
Arguments:
- tokens: bfloat16 [32768, 1024], P(('dp', 'row'), 'col'), may hold values from -6 to 6
- ln1_gain: bfloat16 [1024], P('col'), may hold values from 0.25 to 1.75
- ln1_bias: bfloat16 [1024], P('col'), may hold values from -1.5 to 1.5
- qkv_weight: bfloat16 [1024, 3072], P('col', 'row'), may hold values from -0.1875 to 0.1875
- qkv_bias: bfloat16 [3072], P('row'), may hold values from -2.5 to 2.5
- out_weight: bfloat16 [1024, 1024], P('row', 'col'), may hold values from -0.5 to 0.5
- out_bias: bfloat16 [1024], P('col'), may hold values from -2.5 to 2.5
- ln2_gain: bfloat16 [1024], P('col'), may hold values from 0.25 to 1.75
- ln2_bias: bfloat16 [1024], P('col'), may hold values from -1.5 to 1.5
- up_weight: bfloat16 [1024, 4096], P('col', 'row'), may hold values from -0.1875 to 0.1875
- up_bias: bfloat16 [4096], P('row'), may hold values from -2.5 to 2.5
- down_weight: bfloat16 [4096, 1024], P('row', 'col'), may hold values from -0.09375 to 0.09375
- down_bias: bfloat16 [1024], P('col'), may hold values from -2.5 to 2.5
- cotangent: bfloat16 [32768, 1024], P(('dp', 'row'), 'col'), may hold values from -6 to 6
Outputs:
- output: float32 [32768, 1024], P(('dp', 'row'), 'col')
- input_grad: float32 [32768, 1024], P(('dp', 'row'), 'col')
- ln1_gain_grad: float32 [1024], P('col')
- ln1_bias_grad: float32 [1024], P('col')
- qkv_weight_grad: float32 [1024, 3072], P('col', 'row')
- qkv_bias_grad: float32 [3072], P('row')
- out_weight_grad: float32 [1024, 1024], P('row', 'col')
- out_bias_grad: float32 [1024], P('col')
- ln2_gain_grad: float32 [1024], P('col')
- ln2_bias_grad: float32 [1024], P('col')
- up_weight_grad: float32 [1024, 4096], P('col', 'row')
- up_bias_grad: float32 [4096], P('row')
- down_weight_grad: float32 [4096, 1024], P('row', 'col')
- down_bias_grad: float32 [1024], P('col')
All inputs are finite; a program needn't handle non-finite values.
Results may differ from a plain program's by a relative error of at most 0.02.
Values may be sent and summed in bfloat16 or wider, within the bound.
A program may use at most 256 MiB of HBM per device.

v0:
```python
import math

import jax
import jax.numpy as jnp
from jax import lax
from jax.sharding import PartitionSpec as P

D = 1024
HEADS = 16
HEAD_DIM = 64
SEQ_LEN = 1024


epsilon = 1e-05
masked = -1e30


def bloom_gelu(values):
    return 0.5 * values * (1.0 + jnp.tanh(0.79788456 * values * (1.0 + 0.044715 * values * values)))


def norm_forward(rows, gain, shift):
    middle = lax.psum(jnp.sum(rows, axis=1), "col") / D
    centred = rows - middle[:, None]
    spread = lax.psum(jnp.sum(centred * centred, axis=1), "col") / D
    inverse = lax.rsqrt(spread + epsilon)
    normed = centred * inverse[:, None]
    return (normed, inverse, (normed * gain + shift).astype(jnp.bfloat16))


def norm_backward(grad_rows, normed, inverse, gain):
    scaled = grad_rows * gain
    first, second = lax.psum((jnp.sum(scaled, axis=1), jnp.sum(scaled * normed, axis=1)), "col")
    return inverse[:, None] * (scaled - first[:, None] / D - normed * (second[:, None] / D))


def gather_rows(values):
    return lax.all_gather(values, "row", axis=0, tiled=True)


def gather_cols(values, backward):
    if backward:
        return lax.all_gather(values, "col", axis=0, tiled=True)
    return lax.all_gather(values, "col", axis=0, tiled=True)


def contract_whole(left, right, backward):
    contract = 1 if backward else 0
    return lax.dot_general(
        left, right, (((1,), (contract,)), ((), ())), preferred_element_type=jnp.float32
    )


def sum_cols(left, wide_right, backward):
    swapped = lax.all_to_all(left, "col", split_axis=0, concat_axis=1, tiled=True)
    return contract_whole(swapped, wide_right, backward)


def sum_rows(left, wide_right, backward):
    swapped = lax.all_to_all(left, "row", split_axis=0, concat_axis=1, tiled=True)
    return contract_whole(swapped, wide_right, backward)


def weight_grad(left, grad):
    return lax.dot_general(left, grad, (((0,), (0,)), ((), ())), preferred_element_type=jnp.float32)


def score_block(query_blk, keys, start, slopes):
    scores = jnp.einsum("qhe,khe->hqk", query_blk, keys, preferred_element_type=jnp.float32) * (
        1.0 / math.sqrt(HEAD_DIM)
    )
    shape = (query_blk.shape[0], keys.shape[0])
    offset = (
        lax.broadcasted_iota(jnp.int32, shape, 1)
        - lax.broadcasted_iota(jnp.int32, shape, 0)
        - start
    )
    scores = scores + slopes[:, None, None] * offset.astype(jnp.float32)[None]
    return jnp.where(offset[None] <= 0, scores, masked)


def split_heads(packed):
    heads_here = packed.shape[1] // (3 * HEAD_DIM)
    parted = packed.reshape(packed.shape[0] // SEQ_LEN, SEQ_LEN, heads_here, 3, HEAD_DIM)
    return (parted[:, :, :, 0], parted[:, :, :, 1], parted[:, :, :, 2])


def attention_forward(packed, slopes):
    queries, keys, values = split_heads(packed)
    length = min(512, SEQ_LEN)

    def one_sequence(triple):
        query_seq, key_seq, value_seq = triple

        def one_block(number):
            start = number * length
            query_blk = lax.dynamic_slice_in_dim(query_seq, start, length, 0)
            scores = score_block(query_blk, key_seq, start, slopes)
            highest = jnp.max(scores, axis=2, keepdims=True)
            expo = jnp.exp(scores - highest)
            totals = jnp.sum(expo, axis=2, keepdims=True)
            weights = (expo / totals).astype(jnp.bfloat16)
            context = jnp.einsum(
                "hqk,khe->qhe", weights, value_seq, preferred_element_type=jnp.float32
            )
            return (context.astype(jnp.bfloat16), highest[:, :, 0] + jnp.log(totals[:, :, 0]))

        contexts, logsums = lax.map(one_block, jnp.arange(SEQ_LEN // length, dtype=jnp.int32))
        return (contexts.reshape(SEQ_LEN, -1), logsums)

    contexts, logsums = lax.map(one_sequence, (queries, keys, values))
    return (contexts.reshape(packed.shape[0], -1), logsums)


def attention_backward(packed, logsums, d_context, slopes):
    queries, keys, values = split_heads(packed)
    d_parted = d_context.reshape(keys.shape[0], SEQ_LEN, keys.shape[2], HEAD_DIM)
    length = min(512, SEQ_LEN)
    factor = 1.0 / math.sqrt(HEAD_DIM)

    def one_sequence(bundle):
        query_seq, key_seq, value_seq, d_seq, logsum_seq = bundle

        def one_block(carry, number):
            d_keys, d_values = carry
            start = number * length
            query_blk = lax.dynamic_slice_in_dim(query_seq, start, length, 0)
            d_blk = lax.dynamic_slice_in_dim(d_seq, start, length, 0)
            scores = score_block(query_blk, key_seq, start, slopes)
            weights = jnp.exp(scores - logsum_seq[number][:, :, None])
            d_weights = jnp.einsum(
                "qhe,khe->hqk", d_blk, value_seq, preferred_element_type=jnp.float32
            )
            centre = jnp.sum(weights * d_weights, axis=2, keepdims=True)
            d_scores = (weights * (d_weights - centre)).astype(jnp.bfloat16)
            d_query = (
                jnp.einsum("hqk,khe->qhe", d_scores, key_seq, preferred_element_type=jnp.float32)
                * factor
            )
            d_keys = (
                d_keys
                + jnp.einsum(
                    "hqk,qhe->khe", d_scores, query_blk, preferred_element_type=jnp.float32
                )
                * factor
            )
            d_values = d_values + jnp.einsum(
                "hqk,qhe->khe",
                weights.astype(jnp.bfloat16),
                d_blk,
                preferred_element_type=jnp.float32,
            )
            return ((d_keys, d_values), d_query)

        zeroed = jnp.zeros(key_seq.shape, jnp.float32)
        (d_keys, d_values), d_queries = lax.scan(
            one_block, (zeroed, zeroed), jnp.arange(SEQ_LEN // length, dtype=jnp.int32)
        )
        return jnp.stack((d_queries.reshape(key_seq.shape), d_keys, d_values), axis=2)

    grads = lax.map(one_sequence, (queries, keys, values, d_parted, logsums))
    return grads.reshape(packed.shape[0], -1).astype(jnp.bfloat16)


def shards(
    tokens,
    ln1_gain,
    ln1_bias,
    qkv_weight,
    qkv_bias,
    out_weight,
    out_bias,
    ln2_gain,
    ln2_bias,
    up_weight,
    up_bias,
    down_weight,
    down_bias,
    cotangent,
):
    qkv_cols, up_cols, down_cols, out_cols = (
        lax.all_gather(qkv_weight, "col", axis=0, tiled=True),
        lax.all_gather(up_weight, "col", axis=0, tiled=True),
        lax.all_gather(down_weight, "col", axis=1, tiled=True),
        lax.all_gather(out_weight, "col", axis=1, tiled=True),
    )
    out_rows, down_rows, up_rows, qkv_rows = (
        lax.all_gather(out_weight, "row", axis=0, tiled=True),
        lax.all_gather(down_weight, "row", axis=0, tiled=True),
        lax.all_gather(up_weight, "row", axis=1, tiled=True),
        lax.all_gather(qkv_weight, "row", axis=1, tiled=True),
    )
    inputs = tokens.astype(jnp.float32)
    gain_one = ln1_gain.astype(jnp.float32)
    gain_two = ln2_gain.astype(jnp.float32)
    normed_one, inverse_one, low_one = norm_forward(inputs, gain_one, ln1_bias.astype(jnp.float32))
    rows_one = gather_rows(low_one)
    packed = (sum_cols(rows_one, qkv_cols, False) + qkv_bias.astype(jnp.float32)).astype(
        jnp.bfloat16
    )
    heads_here = packed.shape[1] // (3 * HEAD_DIM)
    head_ids = lax.axis_index("row") * heads_here + jnp.arange(heads_here, dtype=jnp.int32)
    slopes = jnp.exp2(-8.0 * (head_ids.astype(jnp.float32) + 1.0) / HEADS)
    contexts, logsums = attention_forward(packed, slopes)
    context_rows = gather_cols(contexts, False)
    resid = inputs + sum_rows(context_rows, out_rows, False) + out_bias.astype(jnp.float32)
    normed_two, inverse_two, low_two = norm_forward(resid, gain_two, ln2_bias.astype(jnp.float32))
    rows_two = gather_rows(low_two)
    upper = sum_cols(rows_two, up_cols, False) + up_bias.astype(jnp.float32)
    acts = bloom_gelu(upper).astype(jnp.bfloat16)
    act_rows = gather_cols(acts, False)
    output = resid + sum_rows(act_rows, down_rows, False) + down_bias.astype(jnp.float32)
    grad_rows = gather_rows(cotangent)
    d_acts = sum_cols(grad_rows, down_cols, True)
    gelu_pull = jax.vjp(bloom_gelu, upper)[1]
    d_upper = gelu_pull(d_acts)[0].astype(jnp.bfloat16)
    d_upper_rows = gather_cols(d_upper, True)
    d_norm_two = sum_rows(d_upper_rows, up_rows, True)
    d_resid = cotangent.astype(jnp.float32) + norm_backward(
        d_norm_two, normed_two, inverse_two, gain_two
    )
    d_branch_rows = gather_rows(d_resid.astype(jnp.bfloat16))
    d_contexts = sum_cols(d_branch_rows, out_cols, True).astype(jnp.bfloat16)
    d_packed = attention_backward(packed, logsums, d_contexts, slopes)
    d_packed_rows = gather_cols(d_packed, True)
    d_norm_one = sum_rows(d_packed_rows, qkv_rows, True)
    input_grad = d_resid + norm_backward(d_norm_one, normed_one, inverse_one, gain_one)
    weights = (
        lax.psum(weight_grad(rows_one, d_packed_rows).astype(jnp.bfloat16), "dp").astype(
            jnp.float32
        ),
        lax.psum(
            jnp.sum(d_packed_rows, axis=0, dtype=jnp.float32).astype(jnp.bfloat16), "dp"
        ).astype(jnp.float32),
        lax.psum(weight_grad(context_rows, d_branch_rows).astype(jnp.bfloat16), "dp").astype(
            jnp.float32
        ),
        lax.psum(weight_grad(rows_two, d_upper_rows).astype(jnp.bfloat16), "dp").astype(
            jnp.float32
        ),
        lax.psum(
            jnp.sum(d_upper_rows, axis=0, dtype=jnp.float32).astype(jnp.bfloat16), "dp"
        ).astype(jnp.float32),
        lax.psum(weight_grad(act_rows, grad_rows).astype(jnp.bfloat16), "dp").astype(jnp.float32),
    )
    vectors = lax.psum(
        (
            jnp.sum(d_norm_one * normed_one, axis=0),
            jnp.sum(d_norm_one, axis=0),
            jnp.sum(d_resid, axis=0),
            jnp.sum(d_norm_two * normed_two, axis=0),
            jnp.sum(d_norm_two, axis=0),
            jnp.sum(cotangent, axis=0, dtype=jnp.float32),
        ),
        ("dp", "row"),
    )
    return (
        output,
        input_grad,
        vectors[0],
        vectors[1],
        weights[0],
        weights[1],
        weights[2],
        vectors[2],
        vectors[3],
        vectors[4],
        weights[3],
        weights[4],
        weights[5],
        vectors[5],
    )


def solution(mesh):
    placed = (
        P(("dp", "row"), "col"),
        P("col"),
        P("col"),
        P("col", "row"),
        P("row"),
        P("row", "col"),
        P("col"),
        P("col"),
        P("col"),
        P("col", "row"),
        P("row"),
        P("row", "col"),
        P("col"),
        P(("dp", "row"), "col"),
    )
    return jax.shard_map(
        shards,
        mesh=mesh,
        in_specs=placed,
        out_specs=(
            P(("dp", "row"), "col"),
            P(("dp", "row"), "col"),
            P("col"),
            P("col"),
            P("col", "row"),
            P("row"),
            P("row", "col"),
            P("col"),
            P("col"),
            P("col"),
            P("col", "row"),
            P("row"),
            P("row", "col"),
            P("col"),
        ),
        check_vma=False,
    )
```

profile of v0, /device:TPU:0, one launch (start us, length us, event | category | flops | bytes accessed | tf_op | source)
XLA Modules:
  0.0 2266.4 jit_solution(3751096489540832278)
XLA Ops:
  27.1 60.2 %all-gather.16.cloned.1.call-done = bf16[8192,512]{0,1:T(8,128)(2,1)} async-done(((bf16[2048,512]{0,1:T(8,128)(2,1)}), bf16[8192,512]{0,1:T(8,128)(2,1)}) %all-gather.16.cloned.1.call-update) | async-done | bytes 8388624 | tf_op jit(solution)/shard_map/all_gather | solution.py:38
  102.8 45.9 %all-gather.18.cloned.1.call-done = bf16[1024,768]{1,0:T(8,128)(2,1)} async-done(((bf16[512,768]{1,0:T(8,128)(2,1)}), bf16[1024,768]{1,0:T(8,128)(2,1)}) %all-gather.18.cloned.1.call-update) | async-done | bytes 1572880 | tf_op jit(solution)/shard_map/all_gather | solution.py:182
  148.7 63.3 %all-to-all-done = bf16[2,4096,512]{1,2,0:T(8,128)(2,1)} async-done(((bf16[2,4096,512]{1,2,0:T(8,128)(2,1)}), bf16[2,4096,512]{1,2,0:T(8,128)(2,1)}, u32[]{:S(2)}, u32[]{:S(2)}) %all-to-all-start) | async-done | bytes 8388640 | tf_op jit(solution)/shard_map/all_to_all | solution.py:55
  253.4 110.9 %while.54 = (s32[]{:T(128)}, bf16[4,1024,256]{2,1,0:T(8,128)(2,1)}, f32[4,2,4,512]{3,2,1,0:T(4,128)}, bf16[4,1024,4,64]{1,3,2,0:T(8,128)(2,1)}, bf16[4,1024,4,64...) while((s32[]{:T(128)}, bf16[4,1024,256]{2,1,0:T(8,128)(2,1)}, ...), condition=%wide.region_9.10_spmd.clone, body=%wide.region_4.9_spmd.clone.sunk | while | flops 577894400 | bytes 43615732 | solution.py:111
  365.7 54.5 %all-gather.20.cloned.1.call-done = bf16[8192,256]{1,0:T(8,128)(2,1)} async-done(((bf16[4096,256]{1,0:T(8,128)(2,1)}), bf16[8192,256]{1,0:T(8,128)(2,1)}) %all-gather.20.cloned.1.call-update) | async-done | bytes 4194320 | tf_op jit(solution)/shard_map/all_gather | solution.py:44
  425.3 76.0 %all-to-all-done.1 = bf16[4,2048,256]{2,1,0:T(8,128)(2,1)} async-done(((bf16[4,2048,256]{2,1,0:T(8,128)(2,1)}), bf16[4,2048,256]{2,1,0:T(8,128)(2,1)}, u32[]{:S(2)}, u32[]{:S(2)}) %all-to-all-start.1) | async-done | bytes 4194336 | tf_op jit(solution)/shard_map/all_to_all | solution.py:60
  538.8 50.2 %all-gather.24.cloned.1.call-done = bf16[8192,512]{0,1:T(8,128)(2,1)} async-done(((bf16[2048,512]{0,1:T(8,128)(2,1)}), bf16[8192,512]{0,1:T(8,128)(2,1)}) %all-gather.24.cloned.1.call-update) | async-done | bytes 8388624 | tf_op jit(solution)/shard_map/all_gather | solution.py:38
  649.1 44.9 %all-gather.26.cloned.1.call-done = bf16[1024,1024]{1,0:T(8,128)(2,1)} async-done(((bf16[512,1024]{1,0:T(8,128)(2,1)}), bf16[1024,1024]{1,0:T(8,128)(2,1)}) %all-gather.26.cloned.1.call-update) | async-done | bytes 2097168 | tf_op jit(solution)/shard_map/all_gather | solution.py:183
  694.1 75.2 %all-to-all-done.2 = bf16[2,4096,512]{1,2,0:T(8,128)(2,1)} async-done(((bf16[2,4096,512]{1,2,0:T(8,128)(2,1)}), bf16[2,4096,512]{1,2,0:T(8,128)(2,1)}, u32[]{:S(2)}, u32[]{:S(2)}) %all-to-all-start.2) | async-done | bytes 8388640 | tf_op jit(solution)/shard_map/all_to_all | solution.py:55
  785.5 42.5 %fusion.44 = (bf16[4096,1024]{1,0:T(8,128)(2,1)}, bf16[4096,1024]{1,0:T(8,128)(2,1)}) fusion(f32[4096,1024]{1,0:T(8,128)} %fusion.65, f32[1024]{0:T(1024)S(1)} %convert_element_type.135, bf16[4096,1024]{0,1:T(8,128)(2,1)} %bitcast.202, bf16[1024,1024]{1,0:T(8,128)(2,1)} %all-gather.34.cloned.1.call-done), kind=kOutput, calls=%fused_computation.65 | convolution fusion | flops 8698986496 | bytes 44044288 | tf_op jit(solution)/shard_map/dot_general | solution.py:49
  828.0 198.7 %all-gather.36.cloned.1.call-done = bf16[8192,1024]{1,0:T(8,128)(2,1)} async-done(((bf16[4096,1024]{1,0:T(8,128)(2,1)}), bf16[8192,1024]{1,0:T(8,128)(2,1)}) %all-gather.36.cloned.1.call-update) | async-done | bytes 16777232 | tf_op jit(solution)/shard_map/all_gather | solution.py:43
  1058.9 56.8 %all-gather.38.cloned.1.call-done = bf16[512,4096]{1,0:T(8,128)(2,1)} async-done(((bf16[512,1024]{1,0:T(8,128)(2,1)}), bf16[512,4096]{1,0:T(8,128)(2,1)}) %all-gather.38.cloned.1.call-update) | async-done | bytes 4194320 | tf_op jit(solution)/shard_map/all_gather | solution.py:190
  1115.7 145.5 %all-to-all-done.5 = bf16[4,2048,1024]{1,2,0:T(8,128)(2,1)} async-done(((bf16[4,2048,1024]{1,2,0:T(8,128)(2,1)}), bf16[4,2048,1024]{1,2,0:T(8,128)(2,1)}, u32[]{:S(2)}, u32[]{:S(2)}) %all-to-all-start.5) | async-done | bytes 16777248 | tf_op jit(solution)/shard_map/all_to_all | solution.py:60
  1303.6 58.7 %all-gather.40.cloned.1.call-done = bf16[8192,512]{0,1:T(8,128)(2,1)} async-done(((bf16[2048,512]{0,1:T(8,128)(2,1)}), bf16[8192,512]{0,1:T(8,128)(2,1)}) %all-gather.40.cloned.1.call-update) | async-done | bytes 8388624 | tf_op jit(solution)/shard_map/all_gather | solution.py:38
  1377.3 98.5 %all_gather.61 = bf16[256,1024]{1,0:T(8,128)(2,1)S(1)} all-gather(bf16[256,512]{1,0:T(8,128)(2,1)S(1)} %copy-done.8), channel_id=1, replica_groups=mesh['dp'=4,'row'=4,'col'=2] {'col'}, dimensions={1}, use_global_device_ids=true | all-gather | bytes 786432 | tf_op jit(solution)/shard_map/all_gather | solution.py:185
  1493.2 255.5 %while.56 = (s32[]{:T(128)}, bf16[4,1024,4,3,64]{1,4,2,3,0:T(8,128)(2,1)}, bf16[4,1024,4,64]{1,3,2,0:T(8,128)(2,1)}, bf16[4,1024,4,64]{1,3,2,0:T(8,128)(2,1)}, b...) while((s32[]{:T(128)}, ...), condition=%wide.region_22.23_spmd.clone, body=%wide.region_18.22_spmd.clone.sunk | while | flops 1374681088 | bytes 85795456 | solution.py:161
  1498.5 55.9 %while.58 = (s32[]{:T(128)}, f32[1024,4,64]{0,2,1:T(8,128)S(1)}, f32[1024,4,64]{0,2,1:T(8,128)S(1)}, bf16[2,512,4,64]{1,0,3,2:T(2,128)(2,1)}, s32[2]{0:T(128)S(1...) while((s32[]{:T(128)}, f32[1024,4,64]{0,2,1:T(8,128)S(1)}, ...), condition=%wide.region_21.21_spmd.clone, body=%wide.region_19.20_spmd.clone.sunk | while | flops 1369962496 | bytes 76325176 | solution.py:156
  1562.4 55.8 %while.58 = (s32[]{:T(128)}, f32[1024,4,64]{0,2,1:T(8,128)S(1)}, f32[1024,4,64]{0,2,1:T(8,128)S(1)}, bf16[2,512,4,64]{1,0,3,2:T(2,128)(2,1)}, s32[2]{0:T(128)S(1...) while((s32[]{:T(128)}, f32[1024,4,64]{0,2,1:T(8,128)S(1)}, ...), condition=%wide.region_21.21_spmd.clone, body=%wide.region_19.20_spmd.clone.sunk | while | flops 1369962496 | bytes 76325176 | solution.py:156
  1626.1 55.8 %while.58 = (s32[]{:T(128)}, f32[1024,4,64]{0,2,1:T(8,128)S(1)}, f32[1024,4,64]{0,2,1:T(8,128)S(1)}, bf16[2,512,4,64]{1,0,3,2:T(2,128)(2,1)}, s32[2]{0:T(128)S(1...) while((s32[]{:T(128)}, f32[1024,4,64]{0,2,1:T(8,128)S(1)}, ...), condition=%wide.region_21.21_spmd.clone, body=%wide.region_19.20_spmd.clone.sunk | while | flops 1369962496 | bytes 76325176 | solution.py:156
  1689.9 55.8 %while.58 = (s32[]{:T(128)}, f32[1024,4,64]{0,2,1:T(8,128)S(1)}, f32[1024,4,64]{0,2,1:T(8,128)S(1)}, bf16[2,512,4,64]{1,0,3,2:T(2,128)(2,1)}, s32[2]{0:T(128)S(1...) while((s32[]{:T(128)}, f32[1024,4,64]{0,2,1:T(8,128)S(1)}, ...), condition=%wide.region_21.21_spmd.clone, body=%wide.region_19.20_spmd.clone.sunk | while | flops 1369962496 | bytes 76325176 | solution.py:156
  1828.8 85.8 %all-gather.42.cloned.1.call-done = bf16[8192,768]{0,1:T(8,128)(2,1)} async-done(((bf16[4096,768]{0,1:T(8,128)(2,1)}), bf16[8192,768]{0,1:T(8,128)(2,1)}) %all-gather.42.cloned.1.call-update) | async-done | bytes 12582928 | tf_op jit(solution)/shard_map/all_gather | solution.py:43
  1925.6 73.4 %all-to-all-done.3 = bf16[4,2048,1024]{1,2,0:T(8,128)(2,1)} async-done(((bf16[4,2048,1024]{1,2,0:T(8,128)(2,1)}), bf16[4,2048,1024]{1,2,0:T(8,128)(2,1)}, u32[]{:S(2)}, u32[]{:S(2)}) %all-to-all-start.3) | async-done | bytes 16777248 | tf_op jit(solution)/shard_map/all_to_all | solution.py:60
  2074.0 67.6 %all-reduce.7.cloned.1.call-done = (bf16[512,768]{1,0:T(8,128)(2,1)}, bf16[256,512]{1,0:T(8,128)(2,1)}, bf16[512,1024]{1,0:T(8,128)(2,1)}, bf16[1024,512]{1,0:T(8,128)(2,1)}) async-done(((bf16[512,768]{1,0:T(8,128)(2,1)}, bf16[256,512]{1,0:T(8,128)(2,1)}, bf16[512,1024]{1,0:T(8,128)(2,1)}, bf16[1024,512]{1,0:T(8,128)(2,1)}), (bf16[512,768]{1,0:T(8,128)(2,1)}, bf16[256,512]{1,0:T(8,128)(2,1)}, ...) | async-done | bytes 3145744 | tf_op jit(solution)/shard_map/psum | solution.py:229
  2200.7 58.3 %all-reduce = (f32[512]{0:T(512)}, f32[512]{0:T(512)}, f32[512]{0:T(512)}, f32[512]{0:T(512)}, f32[512]{0:T(512)}, /*index=5*/f32[512]{0:T(512)}) all-reduce(f32[512]{0:T(512)S(1)} %get-tuple-element.369, f32[512]{0:T(512)S(1)} %get-tuple-element.477, f32[512]{0:T(512)S(1)} %copy-done.15, ...), channel_id=1, replica_groups=mesh['dp'=4,'row'=4,'col'=2] {'dp','row'}, use_global_device_ids=true, to_apply=%region_28.29 | all-reduce | flops 3072 | bytes 24576 | tf_op jit(solution)/shard_map/psum | solution.py:246
  (418 shorter events, 957.1 us)
Async XLA Ops:
  8.0 79.2 %all-gather.16.cloned.1.call-start = ((), (), s32[]{:S(2)}) async-start(), calls=%async_computation.8 | async-start | bytes 10485760 | tf_op jit(solution)/shard_map/all_gather | solution.py:38
  95.0 117.0 %all-to-all-start = ((bf16[2,4096,512]{1,2,0:T(8,128)(2,1)}), bf16[2,4096,512]{1,2,0:T(8,128)(2,1)}, u32[]{:S(2)}, u32[]{:S(2)}) async-start(bf16[2,4096,512]{1,2,0:T(8,128)(2,1)} %bitcast.190), calls=%async_computation | async-start | bytes 16777216 | tf_op jit(solution)/shard_map/all_to_all | solution.py:55
  102.1 46.6 %all-gather.18.cloned.1.call-start = ((), (), s32[]{:S(2)}) async-start(), calls=%async_computation.9 | async-start | bytes 2359296 | tf_op jit(solution)/shard_map/all_gather | solution.py:182
  102.7 317.5 %all-gather.20.cloned.1.call-start = ((), (), s32[]{:S(2)}) async-start(), calls=%async_computation.10 | async-start | bytes 6291456 | tf_op jit(solution)/shard_map/all_gather | solution.py:44
  364.3 143.3 %all-gather.22.cloned.1.call-start = ((), (), s32[]{:S(2)}) async-start(), calls=%async_computation.11 | async-start | bytes 1310720 | tf_op jit(solution)/shard_map/all_gather | solution.py:188
  364.9 166.8 %all-gather.32.cloned.1.call-start = ((), (), s32[]{:S(2)}) async-start(), calls=%async_computation.16 | async-start | bytes 10485760 | tf_op jit(solution)/shard_map/all_gather | solution.py:38
  420.1 81.2 %all-to-all-start.1 = ((bf16[4,2048,256]{2,1,0:T(8,128)(2,1)}), bf16[4,2048,256]{2,1,0:T(8,128)(2,1)}, u32[]{:S(2)}, u32[]{:S(2)}) async-start(bf16[4,2048,256]{2,1,0:T(8,128)(2,1)} %bitcast.203), calls=%async_computation.1 | async-start | bytes 8388608 | tf_op jit(solution)/shard_map/all_to_all | solution.py:60
  425.2 163.8 %all-gather.24.cloned.1.call-start = ((), (), s32[]{:S(2)}) async-start(), calls=%async_computation.12 | async-start | bytes 10485760 | tf_op jit(solution)/shard_map/all_gather | solution.py:38
  531.7 96.8 %all-to-all-start.4 = ((bf16[2,4096,512]{2,1,0:T(8,128)(2,1)}), bf16[2,4096,512]{2,1,0:T(8,128)(2,1)}, u32[]{:S(2)}, u32[]{:S(2)}) async-start(bf16[2,4096,512]{2,1,0:T(8,128)(2,1)} %bitcast.197), calls=%async_computation.4 | async-start | bytes 16777216 | tf_op jit(solution)/shard_map/all_to_all | solution.py:55
  628.5 140.8 %all-to-all-start.2 = ((bf16[2,4096,512]{1,2,0:T(8,128)(2,1)}), bf16[2,4096,512]{1,2,0:T(8,128)(2,1)}, u32[]{:S(2)}, u32[]{:S(2)}) async-start(bf16[2,4096,512]{1,2,0:T(8,128)(2,1)} %bitcast.191), calls=%async_computation.2 | async-start | bytes 16777216 | tf_op jit(solution)/shard_map/all_to_all | solution.py:55
  635.6 58.5 %all-gather.26.cloned.1.call-start = ((), (), s32[]{:S(2)}) async-start(), calls=%async_computation.13 | async-start | bytes 3145728 | tf_op jit(solution)/shard_map/all_gather | solution.py:183
  636.3 149.1 %all-gather.34.cloned.1.call-start = ((), (), s32[]{:S(2)}) async-start(), calls=%async_computation.17 | async-start | bytes 3145728 | tf_op jit(solution)/shard_map/all_gather | solution.py:184
  636.9 389.8 %all-gather.36.cloned.1.call-start = ((), (), s32[]{:S(2)}) async-start(), calls=%async_computation.18 | async-start | bytes 25165824 | tf_op jit(solution)/shard_map/all_gather | solution.py:43
  1048.5 212.7 %all-to-all-start.5 = ((bf16[4,2048,1024]{1,2,0:T(8,128)(2,1)}), bf16[4,2048,1024]{1,2,0:T(8,128)(2,1)}, u32[]{:S(2)}, u32[]{:S(2)}) async-start(bf16[4,2048,1024]{1,2,0:T(8,128)(2,1)} %copy.85), calls=%async_computation.5 | async-start | bytes 33554432 | tf_op jit(solution)/shard_map/all_to_all | solution.py:60
  1055.7 60.0 %all-gather.38.cloned.1.call-start = ((), (), s32[]{:S(2)}) async-start(), calls=%async_computation.19 | async-start | bytes 5242880 | tf_op jit(solution)/shard_map/all_gather | solution.py:190
  1056.4 305.9 %all-gather.40.cloned.1.call-start = ((), (), s32[]{:S(2)}) async-start(), calls=%async_computation.20 | async-start | bytes 10485760 | tf_op jit(solution)/shard_map/all_gather | solution.py:38
  1370.1 106.2 %all-to-all-start.6 = ((bf16[2,4096,512]{1,2,0:T(8,128)(2,1)}), bf16[2,4096,512]{1,2,0:T(8,128)(2,1)}, u32[]{:S(2)}, u32[]{:S(2)}) async-start(bf16[2,4096,512]{1,2,0:T(8,128)(2,1)} %bitcast.192), calls=%async_computation.6 | async-start | bytes 16777216 | tf_op jit(solution)/shard_map/all_to_all | solution.py:55
  1377.3 385.9 %all-gather.28.cloned.1.call-start = ((), (), s32[]{:S(2)}) async-start(), calls=%async_computation.14 | async-start | bytes 25165824 | tf_op jit(solution)/shard_map/all_gather | solution.py:44
  1475.8 438.8 %all-gather.42.cloned.1.call-start = ((), (), s32[]{:S(2)}) async-start(), calls=%async_computation.21 | async-start | bytes 18874368 | tf_op jit(solution)/shard_map/all_gather | solution.py:43
  1786.3 212.6 %all-to-all-start.3 = ((bf16[4,2048,1024]{1,2,0:T(8,128)(2,1)}), bf16[4,2048,1024]{1,2,0:T(8,128)(2,1)}, u32[]{:S(2)}, u32[]{:S(2)}) async-start(bf16[4,2048,1024]{1,2,0:T(8,128)(2,1)} %copy.81), calls=%async_computation.3 | async-start | bytes 33554432 | tf_op jit(solution)/shard_map/all_to_all | solution.py:60
  1793.4 239.3 %all-gather.30.cloned.1.call-start = ((), (), s32[]{:S(2)}) async-start(), calls=%async_computation.15 | async-start | bytes 5242880 | tf_op jit(solution)/shard_map/all_gather | solution.py:189
  1998.9 161.3 %all-to-all-start.7 = ((bf16[4,2048,768]{1,2,0:T(8,128)(2,1)}), bf16[4,2048,768]{1,2,0:T(8,128)(2,1)}, u32[]{:S(2)}, u32[]{:S(2)}) async-start(bf16[4,2048,768]{1,2,0:T(8,128)(2,1)} %bitcast.189), calls=%async_computation.7 | async-start | bytes 25165824 | tf_op jit(solution)/shard_map/all_to_all | solution.py:60
  2005.3 136.3 %all-reduce.7.cloned.1.call-start = ((), (), s32[]{:S(2)}) async-start(), calls=%async_computation.23 | async-start | bytes 6291456 | tf_op jit(solution)/shard_map/psum | solution.py:229
  2018.9 131.4 %all-gather.44.cloned.1.call-start = ((), (), s32[]{:S(2)}) async-start(), calls=%async_computation.22 | async-start | bytes 3932160 | tf_op jit(solution)/shard_map/all_gather | solution.py:191
  (27 other events, 235.5 us)
Sparse Core Ops, SparseCore 0:
  27.2 60.0 all-gather.15
  1058.1 57.5 all-gather.37
  1303.7 58.5 all-gather.39
  2019.0 122.5 all-reduce.6
Sparse Core Ops, SparseCore 1:
  104.1 44.5 all-gather.17
  364.4 55.6 all-gather.19
  421.6 22.3 all-gather.21
  445.5 80.1 all-gather.31
  531.8 57.2 all-gather.23
  637.9 56.1 all-gather.25
  695.5 55.5 all-gather.33
  828.1 198.6 all-gather.35
  1475.9 197.8 all-gather.27
  1763.2 151.4 all-gather.41
  1916.0 56.9 all-gather.29
  2021.2 45.5 all-gather.43
where the time goes:
time: 2290 us; the launch traced here: 2270 us
  waiting for transfers between devices  1200 us (52%)
  matrix products  327 us (14%)
  local copies, waits for them, and re-layouts  321 us (14%)
  blocking collectives  204 us (9%)
  other arithmetic  113 us (5%)
  starting transfers between devices  55.1 us (2%)
  loops' own time  26.7 us (1%)
    all_gather x4, waiting for transfers between devices, gather_cols(): return lax.all_gather(values, 'col', axis=0, tiled=True)  339 us
    all_to_all x4, waiting for transfers between devices, sum_rows(): lax.all_to_all(left, 'row', split_axis=0, concat_axis=1, tiled=True)  305 us
    all_to_all x4, waiting for transfers between devices, sum_cols(): lax.all_to_all(left, 'col', split_axis=0, concat_axis=1, tiled=True)  170 us
    all_gather x4, waiting for transfers between devices, gather_rows(): return lax.all_gather(values, 'row', axis=0, tiled=True)  169 us
    dot_general x8, matrix products, contract_whole(): lax.dot_general(left, right, (((1,), (contract,)), ((), ())), preferred_e...  126 us
    all_gather x1, blocking collectives, shards(): lax.all_gather(out_weight, 'col', axis=1, tiled=True)  98.5 us
    dynamic_update_slice x16, local copies, waits for them, and re-layouts, one_sequence(): lax.scan(one_block, (zeroed, zeroed), jnp.arange(SEQ_LEN // length, dtype...  81.6 us
    psum x1, waiting for transfers between devices, shards(): lax.psum(weight_grad(rows_one, d_packed_rows).astype(jnp.bfloat16), 'dp')  67.6 us
  transfers between devices with their start and end apart: 24, of which 17 were waited for; matrix products, arithmetic and copies ran while one was open for 20% of the time, Pallas kernels for 0%

commit v1 on v0

--- a/solution.py
+++ b/solution.py
@@ -1,8 +1,11 @@
+import functools
 import math
 
 import jax
 import jax.numpy as jnp
 from jax import lax
+from jax.experimental import pallas as pl
+from jax.experimental.pallas import tpu as pltpu
 from jax.sharding import PartitionSpec as P
 
 D = 1024
@@ -162,7 +165,7 @@
     return grads.reshape(packed.shape[0], -1).astype(jnp.bfloat16)
 
 
-def shards(
+def split_shards(
     tokens,
     ln1_gain,
     ln1_bias,
@@ -272,7 +275,346 @@
     )
 
 
+BLOCK = 256
+NT = (((1,), (1,)), ((), ()))
+NN = (((1,), (0,)), ((), ()))
+TN = (((0,), (0,)), ((), ()))
+
+
+def mm(left, right, dims):
+    return lax.dot_general(left, right, dims, preferred_element_type=jnp.float32)
+
+
+def key_bias(slope, bias_ref):
+    shape = bias_ref.shape
+    bias_ref[...] = lax.broadcasted_iota(jnp.int32, shape, 0).astype(jnp.float32) * slope
+
+
+def scores_t(keys, queries, bias_ref, keep, start, stop):
+    scores = mm(keys[:stop], queries, NT) + bias_ref[:stop]
+    last = jnp.where(keep, scores[start:], masked)
+    return last if start == 0 else jnp.concatenate((scores[:start], last), axis=0)
+
+
+def lower_mask():
+    rows = lax.broadcasted_iota(jnp.int32, (BLOCK, BLOCK), 0)
+    return rows <= lax.broadcasted_iota(jnp.int32, (BLOCK, BLOCK), 1)
+
+
+def forward_kernel(slope_ref, packed_ref, context_ref, lse_ref, bias_ref):
+    pair = pl.program_id(0)
+    keep = lower_mask()
+    for half in range(2):
+        base = 3 * HEAD_DIM * half
+        key_bias(slope_ref[2 * pair + half], bias_ref)
+        queries = packed_ref[:, base : base + 64] * jnp.bfloat16(0.125)
+        keys = packed_ref[:, base + 64 : base + 128]
+        values_t = packed_ref[:, base + 128 : base + 192].T
+        for start in range(0, SEQ_LEN, BLOCK):
+            stop = start + BLOCK
+            scores = scores_t(keys, queries[start:stop], bias_ref, keep, start, stop)
+            highest = jnp.max(scores, axis=0, keepdims=True)
+            expo = jnp.exp(scores - highest)
+            total = jnp.sum(expo, axis=0, keepdims=True)
+            context = mm(values_t[:, :stop], expo.astype(jnp.bfloat16), NN) / total
+            context_ref[start:stop, 64 * half : 64 * half + 64] = context.T.astype(jnp.bfloat16)
+            lse_ref[0, half : half + 1, start:stop] = highest + jnp.log(total)
+
+
+def backward_kernel(
+    slope_ref, packed_ref, d_context_ref, lse_ref, d_packed_ref, bias_ref, d_keys_ref, d_values_ref
+):
+    pair = pl.program_id(0)
+    keep = lower_mask()
+    for half in range(2):
+        base = 3 * HEAD_DIM * half
+        key_bias(slope_ref[2 * pair + half], bias_ref)
+        queries = packed_ref[:, base : base + 64] * jnp.bfloat16(0.125)
+        keys = packed_ref[:, base + 64 : base + 128]
+        values = packed_ref[:, base + 128 : base + 192]
+        keys_t = keys.T
+        d_context = d_context_ref[:, 64 * half : 64 * half + 64]
+        for start in range(SEQ_LEN - BLOCK, -1, -BLOCK):
+            stop = start + BLOCK
+            query_blk = queries[start:stop]
+            d_blk = d_context[start:stop]
+            scores = scores_t(keys, query_blk, bias_ref, keep, start, stop)
+            weights = jnp.exp(scores - lse_ref[0, half : half + 1, start:stop])
+            weighted = weights * mm(values[:stop], d_blk, NT)
+            centre = jnp.sum(weighted, axis=0, keepdims=True)
+            d_scores = (weighted - weights * centre).astype(jnp.bfloat16)
+            d_query = mm(keys_t[:, :stop], d_scores, NN) * 0.125
+            d_packed_ref[start:stop, base : base + 64] = d_query.T.astype(jnp.bfloat16)
+            d_keys = mm(d_scores, query_blk, NN)
+            d_values = mm(weights.astype(jnp.bfloat16), d_blk, NN)
+            if stop == SEQ_LEN:
+                d_keys_ref[...] = d_keys
+                d_values_ref[...] = d_values
+            else:
+                d_keys_ref[:stop] += d_keys
+                d_values_ref[:stop] += d_values
+        d_packed_ref[:, base + 64 : base + 128] = d_keys_ref[...].astype(jnp.bfloat16)
+        d_packed_ref[:, base + 128 : base + 192] = d_values_ref[...].astype(jnp.bfloat16)
+
+
+def fused_forward(packed, slopes):
+    pairs = HEADS // 2
+    return pl.pallas_call(
+        forward_kernel,
+        grid=(pairs,),
+        out_shape=(
+            jax.ShapeDtypeStruct((SEQ_LEN, D), jnp.bfloat16),
+            jax.ShapeDtypeStruct((pairs, 2, SEQ_LEN), jnp.float32),
+        ),
+        in_specs=[
+            pl.BlockSpec(memory_space=pltpu.SMEM),
+            pl.BlockSpec((SEQ_LEN, 384), lambda i: (0, i)),
+        ],
+        out_specs=(
+            pl.BlockSpec((SEQ_LEN, 128), lambda i: (0, i)),
+            pl.BlockSpec((1, 2, SEQ_LEN), lambda i: (i, 0, 0)),
+        ),
+        scratch_shapes=[pltpu.VMEM((SEQ_LEN, BLOCK), jnp.float32)],
+        compiler_params=pltpu.CompilerParams(vmem_limit_bytes=48 * 1024 * 1024),
+        cost_estimate=pl.CostEstimate(
+            flops=4 * HEADS * SEQ_LEN * SEQ_LEN * 256,
+            bytes_accessed=8 * SEQ_LEN * D,
+            transcendentals=HEADS * SEQ_LEN * SEQ_LEN,
+        ),
+        name="attend",
+    )(slopes, packed)
+
+
+def fused_backward(packed, d_context, logsums, slopes):
+    pairs = HEADS // 2
+    return pl.pallas_call(
+        backward_kernel,
+        grid=(pairs,),
+        out_shape=jax.ShapeDtypeStruct((SEQ_LEN, 3 * D), jnp.bfloat16),
+        in_specs=[
+            pl.BlockSpec(memory_space=pltpu.SMEM),
+            pl.BlockSpec((SEQ_LEN, 384), lambda i: (0, i)),
+            pl.BlockSpec((SEQ_LEN, 128), lambda i: (0, i)),
+            pl.BlockSpec((1, 2, SEQ_LEN), lambda i: (i, 0, 0)),
+        ],
+        out_specs=pl.BlockSpec((SEQ_LEN, 384), lambda i: (0, i)),
+        scratch_shapes=[
+            pltpu.VMEM((SEQ_LEN, BLOCK), jnp.float32),
+            pltpu.VMEM((SEQ_LEN, HEAD_DIM), jnp.float32),
+            pltpu.VMEM((SEQ_LEN, HEAD_DIM), jnp.float32),
+        ],
+        compiler_params=pltpu.CompilerParams(vmem_limit_bytes=48 * 1024 * 1024),
+        cost_estimate=pl.CostEstimate(
+            flops=10 * HEADS * SEQ_LEN * SEQ_LEN * 256,
+            bytes_accessed=14 * SEQ_LEN * D,
+            transcendentals=HEADS * SEQ_LEN * SEQ_LEN,
+        ),
+        name="attend_back",
+    )(slopes, packed, d_context, logsums)
+
+
+def local_norm(rows, gain, shift):
+    centred = rows - jnp.mean(rows, axis=1, keepdims=True)
+    inverse = lax.rsqrt(jnp.mean(centred * centred, axis=1, keepdims=True) + epsilon)
+    normed = centred * inverse
+    return (normed, inverse, (normed * gain + shift).astype(jnp.bfloat16))
+
+
+def local_norm_back(grad_rows, normed, inverse, gain):
+    scaled = grad_rows * gain
+    first = jnp.mean(scaled, axis=1, keepdims=True)
+    second = jnp.mean(scaled * normed, axis=1, keepdims=True)
+    return inverse * (scaled - first - normed * second)
+
+
+def swap(value, axis, bit, size):
+    return lax.ppermute(value, axis, [(i, i ^ bit) for i in range(size)])
+
+
+def part(value, index, size, axis):
+    return lax.dynamic_slice_in_dim(value, index * size, size, axis)
+
+
+def whole_weight(weight, rows_on_col):
+    names = ("col", "row") if rows_on_col else ("row", "col")
+    blocks = lax.all_gather(weight, names, axis=0, tiled=False)
+    first, second = (2, 4) if rows_on_col else (4, 2)
+    height, width = weight.shape
+    blocks = blocks.reshape(first, second, height, width)
+    return blocks.transpose(0, 2, 1, 3).reshape(first * height, second * width)
+
+
+def join_cols(mine, theirs, col):
+    return jnp.where(
+        col == 0,
+        jnp.concatenate((mine, theirs), axis=1),
+        jnp.concatenate((theirs, mine), axis=1),
+    )
+
+
+def take_sequence(rows, col):
+    mine = part(rows, col, SEQ_LEN, 0)
+    theirs = swap(part(rows, 1 - col, SEQ_LEN, 0), "col", 1, 2)
+    return join_cols(mine, theirs, col)
+
+
+def give_features(rows, col):
+    half = D // 2
+    mine = part(rows, col, half, 1)
+    sent = part(rows, 1 - col, half, 1).astype(jnp.bfloat16)
+    theirs = swap(sent, "col", 1, 2).astype(jnp.float32)
+    return jnp.where(
+        col == 0,
+        jnp.concatenate((mine, theirs), axis=0),
+        jnp.concatenate((theirs, mine), axis=0),
+    )
+
+
+def halve(total, axis_name, bit, size, index, dim):
+    half = total.shape[dim] // 2
+    theirs = swap(part(total, 1 - index, half, dim), axis_name, bit, size)
+    mine = part(total, index, half, dim)
+    return (mine.astype(jnp.float32) + theirs.astype(jnp.float32)).astype(jnp.bfloat16)
+
+
+def core_columns(values, core):
+    size = values.shape[1] // 4
+    return jnp.concatenate((part(values, core, size, 1), part(values, 2 + core, size, 1)), axis=1)
+
+
+def scattered_grad(left, right, split_right, row, col, x_first):
+    chip, core = row // 2, row % 2
+    if split_right:
+        sent = mm(left, core_columns(right, 1 - core), TN).astype(jnp.bfloat16)
+        own = mm(left, core_columns(right, core), TN)
+    else:
+        sent = mm(core_columns(left, 1 - core), right, TN).astype(jnp.bfloat16)
+        own = mm(core_columns(left, core), right, TN)
+    total = (own + swap(sent, "row", 1, 4).astype(jnp.float32)).astype(jnp.bfloat16)
+    row_dim = 1 if split_right else 0
+    if x_first:
+        total = halve(total, "row", 2, 4, chip, row_dim)
+        return halve(total, "col", 1, 2, col, 1 - row_dim)
+    total = halve(total, "col", 1, 2, col, 1 - row_dim)
+    return halve(total, "row", 2, 4, chip, row_dim)
+
+
+def whole_shards(
+    tokens,
+    ln1_gain,
+    ln1_bias,
+    qkv_weight,
+    qkv_bias,
+    out_weight,
+    out_bias,
+    ln2_gain,
+    ln2_bias,
+    up_weight,
+    up_bias,
+    down_weight,
+    down_bias,
+    cotangent,
+):
+    row, col = lax.axis_index("row"), lax.axis_index("col")
+    inputs = take_sequence(tokens, col).astype(jnp.float32)
+    qkv_all = whole_weight(qkv_weight, True)
+    out_all = whole_weight(out_weight, False)
+    up_all = whole_weight(up_weight, True)
+    down_all = whole_weight(down_weight, False)
+    cot = take_sequence(cotangent, col)
+    wide = lax.all_gather(
+        jnp.concatenate((ln1_gain, ln1_bias, out_bias, ln2_gain, ln2_bias, down_bias)).reshape(
+            6, D // 2
+        ),
+        "col",
+        axis=1,
+        tiled=True,
+    ).astype(jnp.float32)
+    gain_one, shift_one, out_shift, gain_two, shift_two, down_shift = (wide[i] for i in range(6))
+    inner = lax.all_gather(jnp.concatenate((qkv_bias, up_bias)), "row", axis=0, tiled=False).astype(
+        jnp.float32
+    )
+    qkv_width = qkv_bias.shape[0]
+    qkv_shift = inner[:, :qkv_width].reshape(-1)
+    up_shift = inner[:, qkv_width:].reshape(-1)
+
+    normed_one, inverse_one, low_one = local_norm(inputs, gain_one, shift_one)
+    packed = (mm(low_one, qkv_all, NN) + qkv_shift).astype(jnp.bfloat16)
+    slopes = jnp.exp2(-8.0 * (jnp.arange(HEADS, dtype=jnp.float32) + 1.0) / HEADS)
+    contexts, logsums = fused_forward(packed, slopes)
+    resid = inputs + mm(contexts, out_all, NN) + out_shift
+    normed_two, inverse_two, low_two = local_norm(resid, gain_two, shift_two)
+    upper = mm(low_two, up_all, NN) + up_shift
+    acts = bloom_gelu(upper).astype(jnp.bfloat16)
+    down_part = scattered_grad(acts, cot, False, row, col, True)
+    output = give_features(resid + mm(acts, down_all, NN) + down_shift, col)
+    d_acts = mm(cot, down_all, NT)
+    d_upper = jax.vjp(bloom_gelu, upper)[1](d_acts)[0].astype(jnp.bfloat16)
+    up_part = scattered_grad(low_two, d_upper, True, row, col, False)
+    d_norm_two = mm(d_upper, up_all, NT)
+    cot_wide = cot.astype(jnp.float32)
+    d_resid = cot_wide + local_norm_back(d_norm_two, normed_two, inverse_two, gain_two)
+    d_branch = d_resid.astype(jnp.bfloat16)
+    out_part = scattered_grad(contexts, d_branch, False, row, col, True)
+    d_contexts = mm(d_branch, out_all, NT).astype(jnp.bfloat16)
+    d_packed = fused_backward(packed, d_contexts, logsums, slopes)
+    qkv_part = scattered_grad(low_one, d_packed, True, row, col, False)
+    d_norm_one = mm(d_packed, qkv_all, NT)
+    input_grad = give_features(
+        d_resid + local_norm_back(d_norm_one, normed_one, inverse_one, gain_one), col
+    )
+
+    down_grad, up_grad = lax.psum((down_part, up_part), "dp")
+    qkv_part, out_part, down_grad, up_grad = lax.optimization_barrier(
+        (qkv_part, out_part, down_grad, up_grad)
+    )
+    qkv_grad, out_grad = lax.psum((qkv_part, out_part), "dp")
+
+    sums = lax.psum(
+        jnp.concatenate(
+            (
+                jnp.sum(d_norm_one * normed_one, axis=0),
+                jnp.sum(d_norm_one, axis=0),
+                jnp.sum(d_resid, axis=0),
+                jnp.sum(d_norm_two * normed_two, axis=0),
+                jnp.sum(d_norm_two, axis=0),
+                jnp.sum(cot_wide, axis=0),
+                jnp.sum(d_packed, axis=0, dtype=jnp.float32),
+                jnp.sum(d_upper, axis=0, dtype=jnp.float32),
+            )
+        ),
+        ("dp", "row", "col"),
+    )
+    vectors = [part(sums[i * D : (i + 1) * D], col, D // 2, 0) for i in range(6)]
+    qkv_bias_grad = part(sums[6 * D : 9 * D], row, qkv_width, 0)
+    up_bias_grad = part(sums[9 * D :], row, up_bias.shape[0], 0)
+    wide_grads = [item.astype(jnp.float32) for item in (qkv_grad, out_grad, up_grad, down_grad)]
+    return (
+        output,
+        input_grad,
+        vectors[0],
+        vectors[1],
+        wide_grads[0],
+        qkv_bias_grad,
+        wide_grads[1],
+        vectors[2],
+        vectors[3],
+        vectors[4],
+        wide_grads[2],
+        up_bias_grad,
+        wide_grads[3],
+        vectors[5],
+    )
+
+
+def whole_or_split(n_row, n_col, *arrays):
+    if n_row == 4 and n_col == 2 and arrays[0].shape[0] == n_col * SEQ_LEN:
+        return whole_shards(*arrays)
+    return split_shards(*arrays)
+
+
 def solution(mesh):
+    body = functools.partial(whole_or_split, mesh.shape['row'], mesh.shape['col'])
     placed = (
         P(("dp", "row"), "col"),
         P("col"),
@@ -290,7 +632,7 @@
         P(("dp", "row"), "col"),
     )
     return jax.shard_map(
-        shards,
+        body,
         mesh=mesh,
         in_specs=placed,
         out_specs=(

time: 2290 us -> 681 us (0.30)
  waiting for transfers between devices: 1200 us -> 138 us
  local copies, waits for them, and re-layouts: 321 us -> 117 us
  matrix products: 327 us -> 157 us
  blocking collectives: 204 us -> 116 us
  Pallas kernels: 0 us -> 79.7 us
  other arithmetic: 113 us -> 38.2 us
  starting transfers between devices: 55.1 us -> 16.4 us
  loops' own time: 26.7 us -> 0 us
    all_gather x15 -> x4, waiting for transfers between devices: 656 us -> 20.5 us  [whole_weight(): blocks = lax.all_gather(weight, names, axis=0, tiled=False)]
    all_to_all x8 -> x0, waiting for transfers between devices: 475 us -> none  [the longest x4 305 us: sum_rows(): lax.all_to_all(left, 'row', split_axis=0, concat_axis=1, tiled=True)]
    dot_general x68 -> x16, matrix products: 327 us -> 157 us  [mm(): lax.dot_general(left, right, dims, preferred_element_type=jnp.float32)]
    all_to_all x8 -> x0, local copies, waits for them, and re-layouts: 97.7 us -> none  [the longest x4 62.3 us: sum_rows(): lax.all_to_all(left, 'row', split_axis=0, concat_axis=1, tiled=True)]
    dynamic_update_slice x32 -> x0, local copies, waits for them, and re-layouts: 92.8 us -> none  [the longest x16 81.6 us: one_sequence(): lax.scan(one_block, (zeroed, zeroed), jnp.arange(SEQ_LEN // length, dtype...]
    ppermute x0 -> x16, waiting for transfers between devices: none -> 81.3 us  [swap(): return lax.ppermute(value, axis, [(i, i ^ bit) for i in range(size)])]
    pallas_call x0 -> x2, Pallas kernels: none -> 79.7 us  [the longest x1 48.2 us: fused_backward(): pl.pallas_call(backward_kernel, grid=(pairs,), out_shape=jax.ShapeDtypeSt...]
    all_to_all x8 -> x0, starting transfers between devices: 54 us -> none  [the longest x4 28.4 us: sum_cols(): lax.all_to_all(left, 'col', split_axis=0, concat_axis=1, tiled=True)]
  transfers between devices with their start and end apart: 24 -> 22, of which waited for: 17 -> 8; matrix products, arithmetic and copies ran while one was open for 20% -> 36% of each run, Pallas kernels for 0% -> 12%
where the time goes in v1:
time: 681 us; the launch traced here: 678 us
  matrix products  157 us (23%)
  waiting for transfers between devices  138 us (20%)
  local copies, waits for them, and re-layouts  117 us (17%)
  blocking collectives  116 us (17%)
  Pallas kernels  79.7 us (12%)
  other arithmetic  38.2 us (6%)
  starting transfers between devices  16.4 us (2%)
  between operations  15.5 us (2%)
    dot_general x16, matrix products, mm(): lax.dot_general(left, right, dims, preferred_element_type=jnp.float32)  157 us
    ppermute x16, waiting for transfers between devices, swap(): return lax.ppermute(value, axis, [(i, i ^ bit) for i in range(size)])  81.3 us
    psum x1, blocking collectives, whole_shards(): lax.psum(jnp.concatenate((jnp.sum(d_norm_one * normed_one, axis=0), jnp.s...  57.1 us
    all_gather x1, blocking collectives, whole_shards(): lax.all_gather(jnp.concatenate((ln1_gain, ln1_bias, out_bias, ln2_gain, l...  53.6 us
    pallas_call x1, Pallas kernels, fused_backward(): pl.pallas_call(backward_kernel, grid=(pairs,), out_shape=jax.ShapeDtypeSt...  48.2 us
    reshape x4, local copies, waits for them, and re-layouts, whole_weight(): blocks = blocks.reshape(first, second, height, width)  44.1 us
    unnamed x118, local copies, waits for them, and re-layouts  36.4 us
    psum x1, waiting for transfers between devices, whole_shards(): qkv_grad, out_grad = lax.psum((qkv_part, out_part), 'dp')  33.4 us
  transfers between devices with their start and end apart: 22, of which 8 were waited for; matrix products, arithmetic and copies ran while one was open for 36% of the time, Pallas kernels for 12%

profile of v1, /device:TPU:0, one launch (start us, length us, event | category | flops | bytes accessed | tf_op | source)
XLA Modules:
  0.0 677.7 jit_solution(17026844865561640147)
XLA Ops:
  22.8 53.6 %all_gather.33 = bf16[6,1024]{1,0:T(8,128)(2,1)S(1)} all-gather(bf16[6,512]{1,0:T(8,128)(2,1)S(1)} %reshape.97), channel_id=1, replica_groups=mesh['dp'=4,'row'=4,'col'=2] {'col'}, dimensions={1}, use_global_device_ids=true | all-gather | bytes 18432 | tf_op jit(solution)/shard_map/all_gather | solution.py:525
  84.6 19.9 %all-gather.11.cloned.1.call-done = bf16[4096,768]{1,0:T(8,128)(2,1)} async-done(((bf16[512,768]{1,0:T(8,128)(2,1)}), bf16[4096,768]{1,0:T(8,128)(2,1)}) %all-gather.11.cloned.1.call-update) | async-done | bytes 6291472 | tf_op jit(solution)/shard_map/all_gather | solution.py:440
  104.5 10.4 %copy.32 = bf16[2,4,512,768]{3,1,2,0:T(4,128)(2,1)} copy(bf16[2,4,512,768]{3,2,1,0:T(8,128)(2,1)} %bitcast.61) | data formatting | bytes 12582912 | tf_op jit(solution)/shard_map/reshape | solution.py:443
  122.2 9.5 %add_convert_fusion.packed_ref = bf16[1024,3072]{1,0:T(8,128)(2,1)} fusion(f32[3072]{0:T(1024)S(1)} %add.272, bf16[1024,3072]{1,0:T(8,128)(2,1)S(1)} %bitcast.62, f32[1024]{0:T(1024)S(1)} %bitcast.80, f32[1024]{0:T(1024)S(1)} %bitcast.75, f32[1024]{0:T(1024)S(1)} %add_rsqrt_fusion.1, f32[1024]{0:T(1024)S(1)} %broadcast_multiply_fusion.5, ...), kind=kOutput, calls=%fused_computation.12 | convolution fusion | flops 6464471040 | bytes 14708737 | tf_op jit(solution)/shard_map/dot_general | solution.py:285
  131.6 31.5 %attend.1 = (bf16[1024,1024]{1,0:T(8,128)(2,1)S(1)}, f32[8,2,1024]{2,1,0:T(2,128)S(1)}) custom-call(f32[16]{0:T(128)S(1)} %multiply_exponential_fusion.slope_ref, bf16[1024,3072]{1,0:T(8,128)(2,1)} %add_convert_fusion.packed_ref), custom_call_target="tpu_custom_call" | custom-call | flops 17179869184 | bytes 8388608 | tf_op jit(solution)/shard_map/attend/pallas_call | solution.py:362
  171.1 13.4 %copy.34 = bf16[2,4,512,1024]{3,1,2,0:T(4,128)(2,1)} copy(bf16[2,4,512,1024]{3,2,1,0:T(8,128)(2,1)} %bitcast.55) | data formatting | bytes 16777216 | tf_op jit(solution)/shard_map/reshape | solution.py:443
  184.4 12.2 %copy.39 = bf16[128,8,4,1024]{3,1,2,0:T(8,128)(2,1)} copy(bf16[128,8,4,1024]{3,2,1,0:T(4,128)(2,1)} %bitcast.49) | data formatting | bytes 16777216
  196.7 19.7 %multiply_convert_fusion = (bf16[1024,4096]{1,0:T(8,128)(2,1)}, f32[1024,4096]{1,0:T(8,128)}) fusion(f32[4096]{0:T(1024)S(1)} %bitcast.73, bf16[1024,1024]{1,0:T(8,128)(2,1)S(1)} %add_convert_fusion.6, bf16[1024,4096]{1,0:T(8,128)(2,1)} %bitcast.58), kind=kOutput, calls=%fused_computation.8 | convolution fusion | flops 8631877632 | bytes 35667968 | tf_op jit(solution)/shard_map/dot_general | solution.py:285
  217.0 16.6 %copy.35 = bf16[4,2,1024,512]{3,1,2,0:T(2,128)(2,1)} copy(bf16[4,2,1024,512]{3,2,1,0:T(8,128)(2,1)} %bitcast.54) | data formatting | bytes 16777216 | tf_op jit(solution)/shard_map/reshape | solution.py:443
  233.6 9.4 %copy.41 = bf16[512,8,2,512]{3,1,2,0:T(8,128)(2,1)} copy(bf16[512,8,2,512]{3,2,1,0:T(2,128)(2,1)} %bitcast.50) | data formatting | bytes 16777216
  243.0 30.0 %convert_reduce_fusion = (f32[4096]{0:T(1024)}, bf16[1024,4096]{1,0:T(8,128)(2,1)}) fusion(bf16[4096,1024]{1,0:T(8,128)(2,1)} %bitcast.56, bf16[1024,512]{1,0:T(8,128)(2,1)} %collective-permute-done.2, bf16[1024,512]{1,0:T(8,128)(2,1)S(1)} %get-tuple-element.57, pred[]{:T(512)S(6)} %eq.11, f32[1024,4096]{1,0:T(8,128)} %get-tuple-element.76, ...), kind=kOutput, calls=%fused_computation.7 | convolution fusion | flops 8708419584 | bytes 35684352 | tf_op jit(solution)/shard_map/dot_general | solution.py:285
  273.0 15.8 %multiply_reduce_fusion = (f32[1024]{0:T(1024)}, f32[1024]{0:T(1024)S(1)}, f32[1024]{0:T(1024)S(1)}, f32[1024]{0:T(1024)}, f32[1024,1024]{1,0:T(8,128)S(1)}) fusion(f32[1024,1024]{1,0:T(8,128)S(1)} %copy-done.1, f32[1024]{0:T(1024)S(1)} %add_rsqrt_fusion, f32[1024]{0:T(1024)S(1)} %broadcast_multiply_fusion.4, f32[1024]{0:T(1024)S(1)} %bitcast.70, ...), kind=kOutput, calls=%fused_computation.56 | convolution fusion | flops 8599367680 | bytes 25194496 | tf_op jit(solution)/shard_map/dot_general | solution.py:285
  308.5 8.5 %fusion.40 = bf16[2048,1024]{1,0:T(8,128)(2,1)} fusion(bf16[1024,1024]{1,0:T(8,128)(2,1)S(1)} %get-tuple-element.45, bf16[1024,1024]{1,0:T(8,128)(2,1)S(1)} %get-tuple-element.46, bf16[1024,512]{1,0:T(8,128)(2,1)} %collective-permute-done.2, bf16[1024,512]{1,0:T(8,128)(2,1)S(1)} %get-tuple-element.57, pred[]{:T(512)S(6)} %eq.11), kind=kOutput, calls=%fused_computation.63 | convolution fusion | flops 4314890240 | bytes 10485761 | tf_op jit(solution)/shard_map/dot_general | solution.py:285
  327.5 48.2 %attend_back.1 = bf16[1024,3072]{1,0:T(8,128)(2,1)} custom-call(f32[16]{0:T(128)S(1)} %multiply_exponential_fusion.slope_ref, bf16[1024,3072]{1,0:T(8,128)(2,1)} %add_convert_fusion.packed_ref, bf16[1024,1024]{1,0:T(8,128)(2,1)S(1)} %convolution_convert_fusion.1.d_context_ref, f32[8,2,1024]{2,1,0:T(2,128)S(1)} %get-tuple-element.21.lse_ref), custom_call_target="tpu_custom_call" | custom-call | flops 42949672960 | bytes 14680064 | tf_op jit(solution)/shard_map/attend_back/pallas_call | solution.py:390
  386.9 12.4 %fusion.18 = (f32[1024]{0:T(1024)S(1)}, f32[1024]{0:T(1024)S(1)}, f32[1024]{0:T(1024)S(1)}, f32[1024]{0:T(1024)S(1)}, f32[1024,1024]{1,0:T(8,128)}) fusion(f32[1024]{0:T(1024)S(1)} %copy-done.33, f32[1024]{0:T(1024)S(1)} %copy-done.27, bf16[1024,512]{1,0:T(8,128)(2,1)S(1)} %copy-done.3, bf16[1024,512]{1,0:T(8,128)(2,1)S(1)} %copy-done.8, pred[]{:T(512)S(6)} %eq.11, ...), kind=kOutput, calls=%fused_computation.33 | convolution fusion | flops 6462369792 | bytes 18903040 | tf_op jit(solution)/shard_map/dot_general | solution.py:285
  407.7 15.2 %add_add_fusion = f32[1024,1024]{1,0:T(8,128)} fusion(f32[1024,1024]{1,0:T(8,128)S(1)} %copy-done.1, f32[1024]{0:T(1024)S(1)} %bitcast.83, bf16[1024,4096]{1,0:T(8,128)(2,1)} %get-tuple-element.75, bf16[4096,1024]{1,0:T(8,128)(2,1)} %bitcast.57), kind=kOutput, calls=%fused_computation.58 | convolution fusion | flops 8592031744 | bytes 25169920 | tf_op jit(solution)/shard_map/dot_general | solution.py:285
  422.9 6.9 %add_convert_fusion.1 = bf16[1024,2048]{1,0:T(8,128)(2,1)S(1)} fusion(bf16[1024,2048]{1,0:T(8,128)(2,1)} %collective-permute-done.13, bf16[1024,1024]{1,0:T(8,128)(2,1)S(1)} %copy-done.14, bf16[1024,1024]{1,0:T(8,128)(2,1)S(1)} %copy-done.16, bf16[1024,1024]{1,0:T(8,128)(2,1)S(1)} %copy-done.15), kind=kOutput, calls=%fused_computation.13 | convolution fusion | flops 4309647360 | bytes 14680064 | tf_op jit(solution)/shard_map/dot_general | solution.py:285
  432.2 8.8 %add_convert_fusion.2 = bf16[2048,1024]{1,0:T(8,128)(2,1)S(1)} fusion(bf16[2048,1024]{1,0:T(8,128)(2,1)} %collective-permute-done.10, bf16[1024,1024]{1,0:T(8,128)(2,1)} %get-tuple-element.47, bf16[1024,1024]{1,0:T(8,128)(2,1)} %get-tuple-element.44, bf16[1024,512]{1,0:T(8,128)(2,1)} %collective-permute-done.2, ...), kind=kOutput, calls=%fused_computation.14 | convolution fusion | flops 4319084544 | bytes 14680065 | tf_op jit(solution)/shard_map/dot_general | solution.py:285
  451.7 27.4 %collective-permute-done.14 = bf16[512,2048]{1,0:T(8,128)(2,1)} collective-permute-done((bf16[512,2048]{1,0:T(8,128)(2,1)}, bf16[512,2048]{1,0:T(8,128)(2,1)}, u32[]{:S(2)}, u32[]{:S(2)}) %collective-permute-start.14) | collective-permute-done | bytes 2097184 | tf_op jit(solution)/shard_map/ppermute | solution.py:431
  482.6 7.2 %collective-permute-done.11 = bf16[1024,1024]{1,0:T(8,128)(2,1)S(1)} collective-permute-done((bf16[1024,1024]{1,0:T(8,128)(2,1)S(1)}, bf16[1024,1024]{1,0:T(8,128)(2,1)S(1)}, u32[]{:S(2)}, u32[]{:S(2)}) %collective-permute-start.11) | collective-permute-done | bytes 2097184 | tf_op jit(solution)/shard_map/ppermute | solution.py:431
  494.3 16.6 %collective-permute-done.15 = bf16[512,1024]{1,0:T(8,128)(2,1)S(1)} collective-permute-done((bf16[512,1024]{1,0:T(8,128)(2,1)S(1)}, bf16[512,1024]{1,0:T(8,128)(2,1)S(1)}, u32[]{:S(2)}, u32[]{:S(2)}) %collective-permute-start.15) | collective-permute-done | bytes 1048608 | tf_op jit(solution)/shard_map/ppermute | solution.py:431
  524.3 26.4 %collective-permute-done.5 = bf16[512,1536]{1,0:T(8,128)(2,1)S(1)} collective-permute-done((bf16[512,1536]{1,0:T(8,128)(2,1)S(1)}, bf16[512,1536]{1,0:T(8,128)(2,1)S(1)}, u32[]{:S(2)}, u32[]{:S(2)}) %collective-permute-start.5) | collective-permute-done | bytes 1572896 | tf_op jit(solution)/shard_map/ppermute | solution.py:431
  554.5 57.1 %psum.35 = f32[13312]{0:T(1024)S(1)} all-reduce(f32[13312]{0:T(1024)S(1)} %constant_dynamic-update-slice_fusion), channel_id=1, replica_groups=mesh['dp'=4,'row'=4,'col'=2] {'dp','row','col'}, use_global_device_ids=true, to_apply=%region_16.17 | all-reduce | flops 13312 | bytes 106496 | tf_op jit(solution)/shard_map/psum | solution.py:573
  632.8 33.4 %all-reduce.5.cloned.1.call-done = (bf16[512,768]{1,0:T(8,128)(2,1)}, bf16[256,512]{1,0:T(8,128)(2,1)}) async-done(((bf16[512,768]{1,0:T(8,128)(2,1)}, bf16[256,512]{1,0:T(8,128)(2,1)}), (bf16[512,768]{1,0:T(8,128)(2,1)}, bf16[256,512]{1,0:T(8,128)(2,1)})) %all-reduce.5.cloned.1.call-update) | async-done | bytes 1048592 | tf_op jit(solution)/shard_map/psum | solution.py:571
  (238 shorter events, 152.0 us)
Async XLA Ops:
  7.2 71.7 %all-gather.13.cloned.1.call-start = ((), (), s32[]{:S(2)}) async-start(), calls=%async_computation.1 | async-start | bytes 2359296 | tf_op jit(solution)/shard_map/all_gather | solution.py:440
  7.9 96.6 %all-gather.11.cloned.1.call-start = ((), (), s32[]{:S(2)}) async-start(), calls=%async_computation | async-start | bytes 7077888 | tf_op jit(solution)/shard_map/all_gather | solution.py:440
  8.7 162.4 %all-gather.15.cloned.1.call-start = ((), (), s32[]{:S(2)}) async-start(), calls=%async_computation.2 | async-start | bytes 9437184 | tf_op jit(solution)/shard_map/all_gather | solution.py:440
  9.4 207.6 %all-gather.17.cloned.1.call-start = ((), (), s32[]{:S(2)}) async-start(), calls=%async_computation.3 | async-start | bytes 9437184 | tf_op jit(solution)/shard_map/all_gather | solution.py:440
  10.0 603.5 %all-reduce.7.cloned.1.call-start = ((), (), s32[]{:S(2)}) async-start(), calls=%async_computation.5 | async-start | bytes 4194304 | tf_op jit(solution)/shard_map/psum | solution.py:567
  11.3 153.4 %copy-start.2 = (bf16[1024,512]{1,0:T(8,128)(2,1)}, bf16[1024,512]{1,0:T(8,128)(2,1)S(1)}, u32[]{:S(2)}) copy-start(bf16[1024,512]{1,0:T(8,128)(2,1)S(1)} %get-tuple-element.60) | copy-start | bytes 3145732
  11.3 65.7 %collective-permute-start = (bf16[1024,512]{1,0:T(8,128)(2,1)}, bf16[1024,512]{1,0:T(8,128)(2,1)S(1)}, u32[]{:S(2)}, u32[]{:S(2)}) collective-permute-start(bf16[1024,512]{1,0:T(8,128)(2,1)} %get-tuple-element.59), channel_id=1, source_target_pairs={{0,1},{1,0},{2,3},{3,2},{4,5},{5,4},{6,7},{7,6},{8,9},{9,8},{10,11... | collective-permute-start | bytes 3145736 | tf_op jit(solution)/shard_map/ppermute | solution.py:431
  15.3 227.7 %collective-permute-start.2 = (bf16[1024,512]{1,0:T(8,128)(2,1)}, bf16[1024,512]{1,0:T(8,128)(2,1)}, u32[]{:S(2)}, u32[]{:S(2)}) collective-permute-start(bf16[1024,512]{1,0:T(8,128)(2,1)} %get-tuple-element.58), channel_id=1, source_target_pairs={{0,1},{1,0},{2,3},{3,2},{4,5},{5,4},{6,7},{7,6},{8,9},{9,8},{10,11... | collective-permute-start | bytes 3145736 | tf_op jit(solution)/shard_map/ppermute | solution.py:431
  171.0 124.3 %copy-start.13 = (bf16[1024,1024]{1,0:T(8,128)(2,1)}, bf16[1024,1024]{1,0:T(8,128)(2,1)S(1)}, u32[]{:S(2)}) copy-start(bf16[1024,1024]{1,0:T(8,128)(2,1)S(1)} %add_convert_fusion.6) | copy-start | bytes 6291460
  301.8 121.1 %collective-permute-start.13 = (bf16[1024,2048]{1,0:T(8,128)(2,1)}, bf16[1024,2048]{1,0:T(8,128)(2,1)}, u32[]{:S(2)}, u32[]{:S(2)}) collective-permute-start(bf16[1024,2048]{1,0:T(8,128)(2,1)} %fusion.37), channel_id=1, source_target_pairs={{0,2},{2,0},{4,6},{6,4},{1,3},{3,1},{5,7},{7,5},{8,10},{10,8},{12,... | collective-permute-start | bytes 12582920 | tf_op jit(solution)/shard_map/ppermute | solution.py:431
  317.1 115.1 %collective-permute-start.10 = (bf16[2048,1024]{1,0:T(8,128)(2,1)}, bf16[2048,1024]{1,0:T(8,128)(2,1)}, u32[]{:S(2)}, u32[]{:S(2)}) collective-permute-start(bf16[2048,1024]{1,0:T(8,128)(2,1)} %fusion.40), channel_id=1, source_target_pairs={{0,2},{2,0},{4,6},{6,4},{1,3},{3,1},{5,7},{7,5},{8,10},{10,8},{12,... | collective-permute-start | bytes 12582920 | tf_op jit(solution)/shard_map/ppermute | solution.py:431
  327.3 191.2 %collective-permute-start.7 = (bf16[512,1024]{1,0:T(8,128)(2,1)}, bf16[512,1024]{1,0:T(8,128)(2,1)}, u32[]{:S(2)}, u32[]{:S(2)}) collective-permute-start(bf16[512,1024]{1,0:T(8,128)(2,1)} %convolution_convert_fusion.2), channel_id=1, source_target_pairs={{0,2},{2,0},{4,6},{6,4},{1,3},{3,1},{5,7},{7,5},{8,10},{10,8},{12,... | collective-permute-start | bytes 3145736 | tf_op jit(solution)/shard_map/ppermute | solution.py:431
  386.6 58.8 %collective-permute-start.4 = (bf16[1024,1536]{1,0:T(8,128)(2,1)}, bf16[1024,1536]{1,0:T(8,128)(2,1)}, u32[]{:S(2)}, u32[]{:S(2)}) collective-permute-start(bf16[1024,1536]{1,0:T(8,128)(2,1)} %convolution_convert_fusion), channel_id=1, source_target_pairs={{0,2},{2,0},{4,6},{6,4},{1,3},{3,1},{5,7},{7,5},{8,10},{10,8},{12,... | collective-permute-start | bytes 9437192 | tf_op jit(solution)/shard_map/ppermute | solution.py:431
  406.6 214.3 %collective-permute-start.3 = (bf16[1024,512]{1,0:T(8,128)(2,1)}, bf16[1024,512]{1,0:T(8,128)(2,1)}, u32[]{:S(2)}, u32[]{:S(2)}) collective-permute-start(bf16[1024,512]{1,0:T(8,128)(2,1)} %dynamic-slice_convert_fusion), channel_id=1, source_target_pairs={{0,1},{1,0},{2,3},{3,2},{4,5},{5,4},{6,7},{7,6},{8,9},{9,8},{10,11... | collective-permute-start | bytes 3145736 | tf_op jit(solution)/shard_map/ppermute | solution.py:431
  431.3 47.8 %collective-permute-start.14 = (bf16[512,2048]{1,0:T(8,128)(2,1)}, bf16[512,2048]{1,0:T(8,128)(2,1)}, u32[]{:S(2)}, u32[]{:S(2)}) collective-permute-start(bf16[512,2048]{1,0:T(8,128)(2,1)} %constant_dynamic-slice_fusion.1), channel_id=1, source_target_pairs={{0,1},{1,0},{2,3},{3,2},{4,5},{5,4},{6,7},{7,6},{8,9},{9,8},{10,11... | collective-permute-start | bytes 6291464 | tf_op jit(solution)/shard_map/ppermute | solution.py:431
  441.2 48.6 %collective-permute-start.11 = (bf16[1024,1024]{1,0:T(8,128)(2,1)S(1)}, bf16[1024,1024]{1,0:T(8,128)(2,1)S(1)}, u32[]{:S(2)}, u32[]{:S(2)}) collective-permute-start(bf16[1024,1024]{1,0:T(8,128)(2,1)S(1)} %constant_dynamic-slice_fusion.7), channel_id=1, source_target_pairs={{0,4},{2,6},{4,0},{6,2},{1,5},{3,7},{5,1},{7,3},{8,12},{10,14},{12... | collective-permute-start | bytes 6291464 | tf_op jit(solution)/shard_map/ppermute | solution.py:431
  481.6 29.4 %collective-permute-start.15 = (bf16[512,1024]{1,0:T(8,128)(2,1)S(1)}, bf16[512,1024]{1,0:T(8,128)(2,1)S(1)}, u32[]{:S(2)}, u32[]{:S(2)}) collective-permute-start(bf16[512,1024]{1,0:T(8,128)(2,1)S(1)} %constant_dynamic-slice_fusion), channel_id=1, source_target_pairs={{0,4},{2,6},{4,0},{6,2},{1,5},{3,7},{5,1},{7,3},{8,12},{10,14},{12... | collective-permute-start | bytes 3145736 | tf_op jit(solution)/shard_map/ppermute | solution.py:431
  490.9 26.2 %collective-permute-start.12 = (bf16[1024,512]{1,0:T(8,128)(2,1)S(1)}, bf16[1024,512]{1,0:T(8,128)(2,1)S(1)}, u32[]{:S(2)}, u32[]{:S(2)}) collective-permute-start(bf16[1024,512]{1,0:T(8,128)(2,1)S(1)} %constant_dynamic-slice_fusion.6), channel_id=1, source_target_pairs={{0,1},{1,0},{2,3},{3,2},{4,5},{5,4},{6,7},{7,6},{8,9},{9,8},{10,11... | collective-permute-start | bytes 3145736 | tf_op jit(solution)/shard_map/ppermute | solution.py:431
  492.2 58.6 %collective-permute-start.5 = (bf16[512,1536]{1,0:T(8,128)(2,1)S(1)}, bf16[512,1536]{1,0:T(8,128)(2,1)S(1)}, u32[]{:S(2)}, u32[]{:S(2)}) collective-permute-start(bf16[512,1536]{1,0:T(8,128)(2,1)S(1)} %constant_dynamic-slice_fusion.19), channel_id=1, source_target_pairs={{0,1},{1,0},{2,3},{3,2},{4,5},{5,4},{6,7},{7,6},{8,9},{9,8},{10,11... | collective-permute-start | bytes 4718600 | tf_op jit(solution)/shard_map/ppermute | solution.py:431
  511.0 111.4 %collective-permute-start.1 = (bf16[1024,512]{1,0:T(8,128)(2,1)}, bf16[1024,512]{1,0:T(8,128)(2,1)}, u32[]{:S(2)}, u32[]{:S(2)}) collective-permute-start(bf16[1024,512]{1,0:T(8,128)(2,1)} %dynamic-slice_convert_fusion.1), channel_id=1, source_target_pairs={{0,1},{1,0},{2,3},{3,2},{4,5},{5,4},{6,7},{7,6},{8,9},{9,8},{10,11... | collective-permute-start | bytes 3145736 | tf_op jit(solution)/shard_map/ppermute | solution.py:431
  518.5 147.8 %all-reduce.5.cloned.1.call-start = ((), (), s32[]{:S(2)}) async-start(), calls=%async_computation.4 | async-start | bytes 2097152 | tf_op jit(solution)/shard_map/psum | solution.py:571
  522.8 30.8 %collective-permute-start.8 = (bf16[256,1024]{1,0:T(8,128)(2,1)S(1)}, bf16[256,1024]{1,0:T(8,128)(2,1)S(1)}, u32[]{:S(2)}, u32[]{:S(2)}) collective-permute-start(bf16[256,1024]{1,0:T(8,128)(2,1)S(1)} %constant_dynamic-slice_fusion.13), channel_id=1, source_target_pairs={{0,4},{2,6},{4,0},{6,2},{1,5},{3,7},{5,1},{7,3},{8,12},{10,14},{12... | collective-permute-start | bytes 1572872 | tf_op jit(solution)/shard_map/ppermute | solution.py:431
  552.1 60.3 %collective-permute-start.6 = (bf16[512,768]{1,0:T(8,128)(2,1)}, bf16[512,768]{1,0:T(8,128)(2,1)S(1)}, u32[]{:S(2)}, u32[]{:S(2)}) collective-permute-start(bf16[512,768]{1,0:T(8,128)(2,1)} %constant_dynamic-slice_fusion.18), channel_id=1, source_target_pairs={{0,4},{2,6},{4,0},{6,2},{1,5},{3,7},{5,1},{7,3},{8,12},{10,14},{12... | collective-permute-start | bytes 2359304 | tf_op jit(solution)/shard_map/ppermute | solution.py:431
  553.8 57.8 %collective-permute-start.9 = (bf16[256,512]{1,0:T(8,128)(2,1)S(1)}, bf16[256,512]{1,0:T(8,128)(2,1)S(1)}, u32[]{:S(2)}, u32[]{:S(2)}) collective-permute-start(bf16[256,512]{1,0:T(8,128)(2,1)S(1)} %constant_dynamic-slice_fusion.12), channel_id=1, source_target_pairs={{0,1},{1,0},{2,3},{3,2},{4,5},{5,4},{6,7},{7,6},{8,9},{9,8},{10,11... | collective-permute-start | bytes 786440 | tf_op jit(solution)/shard_map/ppermute | solution.py:431
  (47 other events, 641.1 us)
Sparse Core Ops, SparseCore 0:
  9.9 39.2 all-gather.12
  51.1 53.3 all-gather.10
  106.4 54.3 all-gather.14
  162.5 54.3 all-gather.16
  518.6 88.0 all-reduce.6
  613.6 52.6 all-reduce.4

commit v2 on v1

--- a/solution.py
+++ b/solution.py
@@ -436,12 +436,38 @@
 
 
 def whole_weight(weight, rows_on_col):
-    names = ("col", "row") if rows_on_col else ("row", "col")
-    blocks = lax.all_gather(weight, names, axis=0, tiled=False)
-    first, second = (2, 4) if rows_on_col else (4, 2)
+    names, bands = (("row", "col"), 4) if rows_on_col else (("col", "row"), 2)
+    blocks = lax.all_gather(weight, names, axis=0, tiled=True)
+    height = blocks.shape[0] // bands
+    return jnp.concatenate([blocks[i * height : (i + 1) * height] for i in range(bands)], axis=1)
+
+
+def whole_qkv(weight, wide, inner):
     height, width = weight.shape
-    blocks = blocks.reshape(first, second, height, width)
-    return blocks.transpose(0, 2, 1, 3).reshape(first * height, second * width)
+    small = jnp.concatenate((wide, inner))
+    rows = -(-small.shape[0] // (16 * width)) * 16
+    small = jnp.pad(small, (0, rows * width - small.shape[0])).reshape(rows, width)
+    blocks = lax.all_gather(
+        jnp.concatenate((weight, small), axis=0), ("row", "col"), axis=0, tiled=False
+    ).reshape(4, 2, height + rows, width)
+    whole = jnp.concatenate(
+        [
+            jnp.concatenate([blocks[r, c, :height] for c in range(2)], axis=0)
+            for r in range(4)
+        ],
+        axis=1,
+    )
+    tails = blocks[:, :, height:].reshape(4, 2, -1).astype(jnp.float32)
+    size = wide.shape[0]
+    wides = tails[0, :, :size].reshape(2, 6, -1).transpose(1, 0, 2).reshape(6, -1)
+    return (whole, wides, tails[:, 0, size : size + inner.shape[0]])
+
+
+def sum_everywhere(vector, n_dp):
+    for axis, size, bits in (("row", 4, (1, 2)), ("col", 2, (1,)), ("dp", n_dp, (1, 2))):
+        for bit in bits:
+            vector = vector + swap(vector, axis, bit, size)
+    return vector
 
 
 def join_cols(mine, theirs, col):
@@ -500,6 +526,7 @@
 
 
 def whole_shards(
+    n_dp,
     tokens,
     ln1_gain,
     ln1_bias,
@@ -517,23 +544,16 @@
 ):
     row, col = lax.axis_index("row"), lax.axis_index("col")
     inputs = take_sequence(tokens, col).astype(jnp.float32)
-    qkv_all = whole_weight(qkv_weight, True)
+    qkv_all, wide, inner = whole_qkv(
+        qkv_weight,
+        jnp.concatenate((ln1_gain, ln1_bias, out_bias, ln2_gain, ln2_bias, down_bias)),
+        jnp.concatenate((qkv_bias, up_bias)),
+    )
     out_all = whole_weight(out_weight, False)
     up_all = whole_weight(up_weight, True)
     down_all = whole_weight(down_weight, False)
     cot = take_sequence(cotangent, col)
-    wide = lax.all_gather(
-        jnp.concatenate((ln1_gain, ln1_bias, out_bias, ln2_gain, ln2_bias, down_bias)).reshape(
-            6, D // 2
-        ),
-        "col",
-        axis=1,
-        tiled=True,
-    ).astype(jnp.float32)
     gain_one, shift_one, out_shift, gain_two, shift_two, down_shift = (wide[i] for i in range(6))
-    inner = lax.all_gather(jnp.concatenate((qkv_bias, up_bias)), "row", axis=0, tiled=False).astype(
-        jnp.float32
-    )
     qkv_width = qkv_bias.shape[0]
     qkv_shift = inner[:, :qkv_width].reshape(-1)
     up_shift = inner[:, qkv_width:].reshape(-1)
@@ -557,20 +577,21 @@
     d_branch = d_resid.astype(jnp.bfloat16)
     out_part = scattered_grad(contexts, d_branch, False, row, col, True)
     d_contexts = mm(d_branch, out_all, NT).astype(jnp.bfloat16)
+    d_contexts, down_part = lax.optimization_barrier((d_contexts, down_part))
+    down_grad = lax.psum(down_part, "dp")
     d_packed = fused_backward(packed, d_contexts, logsums, slopes)
+    d_packed, up_part, down_grad = lax.optimization_barrier((d_packed, up_part, down_grad))
+    up_grad = lax.psum(up_part, "dp")
     qkv_part = scattered_grad(low_one, d_packed, True, row, col, False)
     d_norm_one = mm(d_packed, qkv_all, NT)
     input_grad = give_features(
         d_resid + local_norm_back(d_norm_one, normed_one, inverse_one, gain_one), col
     )
 
-    down_grad, up_grad = lax.psum((down_part, up_part), "dp")
-    qkv_part, out_part, down_grad, up_grad = lax.optimization_barrier(
-        (qkv_part, out_part, down_grad, up_grad)
-    )
+    qkv_part, out_part, up_grad = lax.optimization_barrier((qkv_part, out_part, up_grad))
     qkv_grad, out_grad = lax.psum((qkv_part, out_part), "dp")
 
-    sums = lax.psum(
+    sums = sum_everywhere(
         jnp.concatenate(
             (
                 jnp.sum(d_norm_one * normed_one, axis=0),
@@ -583,7 +604,7 @@
                 jnp.sum(d_upper, axis=0, dtype=jnp.float32),
             )
         ),
-        ("dp", "row", "col"),
+        n_dp,
     )
     vectors = [part(sums[i * D : (i + 1) * D], col, D // 2, 0) for i in range(6)]
     qkv_bias_grad = part(sums[6 * D : 9 * D], row, qkv_width, 0)
@@ -607,14 +628,14 @@
     )
 
 
-def whole_or_split(n_row, n_col, *arrays):
-    if n_row == 4 and n_col == 2 and arrays[0].shape[0] == n_col * SEQ_LEN:
-        return whole_shards(*arrays)
+def whole_or_split(n_dp, n_row, n_col, *arrays):
+    if n_dp == 4 and n_row == 4 and n_col == 2 and arrays[0].shape[0] == n_col * SEQ_LEN:
+        return whole_shards(n_dp, *arrays)
     return split_shards(*arrays)
 
 
 def solution(mesh):
-    body = functools.partial(whole_or_split, mesh.shape['row'], mesh.shape['col'])
+    body = functools.partial(whole_or_split, *(mesh.shape[name] for name in ('dp', 'row', 'col')))
     placed = (
         P(("dp", "row"), "col"),
         P("col"),

time: 681 us -> 637 us (0.935)
  blocking collectives: 116 us -> 0 us
  waiting for transfers between devices: 138 us -> 224 us
  local copies, waits for them, and re-layouts: 117 us -> 71.3 us
  matrix products: 157 us -> 174 us
  other arithmetic: 38.2 us -> 48.2 us
    all_gather x2 -> x0, blocking collectives: 58.8 us -> none  [the longest x1 53.6 us: whole_shards(): lax.all_gather(jnp.concatenate((ln1_gain, ln1_bias, out_bias, ln2_gain, l...]
    psum x1 -> x0, blocking collectives: 57.1 us -> none  [whole_shards(): lax.psum(jnp.concatenate((jnp.sum(d_norm_one * normed_one, axis=0), jnp.s...]
    ppermute x16 -> x21, waiting for transfers between devices: 81.3 us -> 131 us  [swap(): return lax.ppermute(value, axis, [(i, i ^ bit) for i in range(size)])]
    reshape x5 -> x1, local copies, waits for them, and re-layouts: 44.1 us -> 0.05 us  [whole_qkv(): jnp.pad(small, (0, rows * width - small.shape[0])).reshape(rows, width)]
    all_gather x4, waiting for transfers between devices: 20.5 us -> 63.4 us  [the longest x1 46.3 us: whole_qkv(): lax.all_gather(jnp.concatenate((weight, small), axis=0), ('row', 'col'),...]
    unnamed x118 -> x135, local copies, waits for them, and re-layouts: 36.4 us -> 15.6 us
    dot_general x16, matrix products: 157 us -> 174 us  [mm(): lax.dot_general(left, right, dims, preferred_element_type=jnp.float32)]
    slice x0 -> x5, local copies, waits for them, and re-layouts: none -> 15.2 us  [the longest x3 13.6 us: whole_weight(): blocks[i * height:(i + 1) * height]]
  transfers between devices with their start and end apart: 22 -> 28, of which waited for: 8 -> 12; matrix products, arithmetic and copies ran while one was open for 36% -> 38% of each run, Pallas kernels for 12% -> 13%
where the time goes in v2:
time: 637 us; the launch traced here: 633 us
  waiting for transfers between devices  224 us (35%)
  matrix products  174 us (27%)
  Pallas kernels  80.5 us (13%)
  local copies, waits for them, and re-layouts  71.3 us (11%)
  other arithmetic  48.2 us (8%)
  starting transfers between devices  19.9 us (3%)
  between operations  15.3 us (2%)
    dot_general x16, matrix products, mm(): lax.dot_general(left, right, dims, preferred_element_type=jnp.float32)  174 us
    ppermute x21, waiting for transfers between devices, swap(): return lax.ppermute(value, axis, [(i, i ^ bit) for i in range(size)])  131 us
    pallas_call x1, Pallas kernels, fused_backward(): pl.pallas_call(backward_kernel, grid=(pairs,), out_shape=jax.ShapeDtypeSt...  48.4 us
    all_gather x1, waiting for transfers between devices, whole_qkv(): lax.all_gather(jnp.concatenate((weight, small), axis=0), ('row', 'col'),...  46.3 us
    pallas_call x1, Pallas kernels, fused_forward(): pl.pallas_call(forward_kernel, grid=(pairs,), out_shape=(jax.ShapeDtypeSt...  32 us
    dynamic_slice x24, local copies, waits for them, and re-layouts, part(): return lax.dynamic_slice_in_dim(value, index * size, size, axis)  28.3 us
    psum x1, waiting for transfers between devices, whole_shards(): qkv_grad, out_grad = lax.psum((qkv_part, out_part), 'dp')  26.9 us
    ppermute x21, starting transfers between devices, swap(): return lax.ppermute(value, axis, [(i, i ^ bit) for i in range(size)])  19.6 us
  transfers between devices with their start and end apart: 28, of which 12 were waited for; matrix products, arithmetic and copies ran while one was open for 38% of the time, Pallas kernels for 13%

profile of v2, /device:TPU:0, one launch (start us, length us, event | category | flops | bytes accessed | tf_op | source)
XLA Modules:
  0.0 633.3 jit_solution(7891936202177228969)
XLA Ops:
  24.5 29.5 %collective-permute-done = bf16[1024,512]{1,0:T(8,128)(2,1)S(1)} collective-permute-done((bf16[1024,512]{1,0:T(8,128)(2,1)}, bf16[1024,512]{1,0:T(8,128)(2,1)S(1)}, u32[]{:S(2)}, u32[]{:S(2)}) %collective-permute-start) | collective-permute-done | bytes 1048608 | tf_op jit(solution)/shard_map/ppermute | solution.py:431
  59.5 46.3 %all-gather.12.cloned.1.call-done = bf16[4224,768]{1,0:T(8,128)(2,1)} async-done(((bf16[528,768]{1,0:T(8,128)(2,1)}), bf16[4224,768]{1,0:T(8,128)(2,1)}) %all-gather.12.cloned.1.call-update) | async-done | bytes 6488080 | tf_op jit(solution)/shard_map/all_gather | solution.py:450
  111.8 5.7 slice_bitcast_fusion.7
  117.5 16.6 %add_convert_fusion.packed_ref = bf16[1024,3072]{1,0:T(8,128)(2,1)} fusion(f32[3072]{0:T(1024)S(1)} %add.287, f32[1024]{0:T(1024)S(1)} %bitcast.61, f32[1024]{0:T(1024)S(1)} %bitcast.56, f32[1024]{0:T(1024)S(1)} %add_rsqrt_fusion.1, f32[1024]{0:T(1024)S(1)} %broadcast_multiply_fusion.5, bf16[512,768]{1,0:T(8,128)(2,1)} %get-tuple-element.61, ...), kind=kOutput, calls=%fused_computation.12 | convolution fusion | flops 6514802688 | bytes 14708737 | tf_op jit(solution)/shard_map/dot_general | solution.py:285
  134.1 32.0 %attend.1 = (bf16[1024,1024]{1,0:T(8,128)(2,1)S(1)}, f32[8,2,1024]{2,1,0:T(2,128)S(1)}) custom-call(f32[16]{0:T(128)S(1)} %multiply_exponential_fusion.slope_ref, bf16[1024,3072]{1,0:T(8,128)(2,1)} %add_convert_fusion.packed_ref), custom_call_target="tpu_custom_call" | custom-call | flops 17179869184 | bytes 8388608 | tf_op jit(solution)/shard_map/attend/pallas_call | solution.py:362
  173.9 6.7 %fusion.92 = (bf16[1024,1024]{1,0:T(8,128)(2,1)}, bf16[1024,1024]{1,0:T(8,128)(2,1)}, bf16[1024,1024]{1,0:T(8,128)(2,1)}, bf16[1024,1024]{1,0:T(8,128)(2,1)}) fusion(bf16[4096,1024]{1,0:T(8,128)(2,1)} %all-gather.8.cloned.1.call-done), kind=kLoop, calls=%fused_computation.182 | loop fusion | bytes 16777216 | tf_op jit(solution)/shard_map/slice | solution.py:442
  180.6 20.6 %multiply_convert_fusion = (bf16[1024,4096]{1,0:T(8,128)(2,1)}, f32[1024,4096]{1,0:T(8,128)}) fusion(f32[4096]{0:T(1024)S(1)} %bitcast.54, bf16[1024,1024]{1,0:T(8,128)(2,1)S(1)} %add_convert_fusion.6, bf16[1024,1024]{1,0:T(8,128)(2,1)} %get-tuple-element.57, bf16[1024,1024]{1,0:T(8,128)(2,1)} %get-tuple-element.58, ...), kind=kOutput, calls=%fused_computation.8 | convolution fusion | flops 8665432064 | bytes 35667968 | tf_op jit(solution)/shard_map/dot_general | solution.py:285
  201.2 17.0 %all-gather.10.cloned.1.call-done = bf16[8192,512]{1,0:T(8,128)(2,1)} async-done(((bf16[1024,512]{1,0:T(8,128)(2,1)}), bf16[8192,512]{1,0:T(8,128)(2,1)}) %all-gather.10.cloned.1.call-update) | async-done | bytes 8388624 | tf_op jit(solution)/shard_map/all_gather | solution.py:440
  222.0 30.1 %convert_reduce_fusion = (f32[4096]{0:T(1024)}, bf16[1024,4096]{1,0:T(8,128)(2,1)S(1)}) fusion(bf16[4096,512]{1,0:T(8,128)(2,1)S(1)} %get-tuple-element.55, bf16[4096,512]{1,0:T(8,128)(2,1)S(1)} %get-tuple-element.54, bf16[1024,512]{1,0:T(8,128)(2,1)} %collective-permute-done.2, bf16[1024,512]{1,0:T(8,128)(2,1)S(1)} %get-tuple-element.77, pred[]{:T(512)S(6)} %eq.11, ...), kind=kOutput, calls=%fused_computation.7 | convolution fusion | flops 8725196800 | bytes 35684352 | tf_op jit(solution)/shard_map/dot_general | solution.py:285
  257.0 6.8 %fusion.39 = bf16[1024,2048]{1,0:T(8,128)(2,1)} fusion(bf16[1024,1024]{1,0:T(8,128)(2,1)S(1)} %copy-done.19, bf16[1024,1024]{1,0:T(8,128)(2,1)S(1)} %get-tuple-element.47, bf16[1024,1024]{1,0:T(8,128)(2,1)S(1)} %get-tuple-element.48), kind=kOutput, calls=%fused_computation.67 | convolution fusion | flops 4305453056 | bytes 10485760 | tf_op jit(solution)/shard_map/dot_general | solution.py:285
  267.2 8.7 %fusion.42 = bf16[2048,1024]{1,0:T(8,128)(2,1)} fusion(bf16[1024,1024]{1,0:T(8,128)(2,1)S(1)} %get-tuple-element.51, bf16[1024,1024]{1,0:T(8,128)(2,1)S(1)} %get-tuple-element.52, bf16[1024,512]{1,0:T(8,128)(2,1)} %collective-permute-done.2, bf16[1024,512]{1,0:T(8,128)(2,1)S(1)} %get-tuple-element.77, pred[]{:T(512)S(6)} %eq.11), kind=kOutput, calls=%fused_computation.68 | convolution fusion | flops 4314890240 | bytes 10485761 | tf_op jit(solution)/shard_map/dot_general | solution.py:285
  276.1 16.1 %multiply_reduce_fusion = (f32[1024]{0:T(1024)}, f32[1024]{0:T(1024)S(1)}, f32[1024]{0:T(1024)S(1)}, f32[1024]{0:T(1024)}, f32[1024,1024]{1,0:T(8,128)S(1)}) fusion(f32[1024,1024]{1,0:T(8,128)} %copy-done, f32[1024]{0:T(1024)S(1)} %add_rsqrt_fusion, f32[1024]{0:T(1024)S(1)} %broadcast_multiply_fusion.4, f32[1024]{0:T(1024)S(1)} %bitcast.51, ...), kind=kOutput, calls=%fused_computation.59 | convolution fusion | flops 8632922112 | bytes 25194496 | tf_op jit(solution)/shard_map/dot_general | solution.py:285
  302.5 6.9 %add_convert_fusion.1 = bf16[1024,2048]{1,0:T(8,128)(2,1)S(1)} fusion(bf16[1024,2048]{1,0:T(8,128)(2,1)} %collective-permute-done.6, bf16[1024,1024]{1,0:T(8,128)(2,1)S(1)} %copy-done.20, bf16[1024,1024]{1,0:T(8,128)(2,1)S(1)} %copy-done.24, bf16[1024,1024]{1,0:T(8,128)(2,1)S(1)} %copy-done.23), kind=kOutput, calls=%fused_computation.15 | convolution fusion | flops 4309647360 | bytes 14680064 | tf_op jit(solution)/shard_map/dot_general | solution.py:285
  312.4 9.8 %add_convert_fusion.2 = bf16[2048,1024]{1,0:T(8,128)(2,1)} fusion(bf16[2048,1024]{1,0:T(8,128)(2,1)} %collective-permute-done.3, bf16[1024,1024]{1,0:T(8,128)(2,1)S(1)} %copy-done.22, bf16[1024,1024]{1,0:T(8,128)(2,1)S(1)} %copy-done.21, bf16[1024,512]{1,0:T(8,128)(2,1)} %collective-permute-done.2, bf16[1024,512]{1,0:T(8,128)(2,1)S(1)} %get-tuple-element.77, ...), kind=kOutput, calls=%fused_computation.16 | convolution fusion | flops 4319084544 | bytes 14680065 | tf_op jit(solution)/shard_map/dot_general | solution.py:285
  326.9 15.1 %add_add_fusion = f32[1024,1024]{1,0:T(8,128)} fusion(f32[1024,1024]{1,0:T(8,128)S(1)} %copy-done.1, f32[1024]{0:T(1024)S(1)} %bitcast.64, bf16[1024,4096]{1,0:T(8,128)(2,1)} %get-tuple-element.97, bf16[4096,512]{1,0:T(8,128)(2,1)} %copy-done.16, bf16[4096,512]{1,0:T(8,128)(2,1)} %copy-done.15), kind=kOutput, calls=%fused_computation.63 | convolution fusion | flops 8608808960 | bytes 25169920 | tf_op jit(solution)/shard_map/dot_general | solution.py:285
  349.8 23.7 %collective-permute-done.4 = bf16[1024,1024]{1,0:T(8,128)(2,1)} collective-permute-done((bf16[1024,1024]{1,0:T(8,128)(2,1)}, bf16[1024,1024]{1,0:T(8,128)(2,1)}, u32[]{:S(2)}, u32[]{:S(2)}) %collective-permute-start.4) | collective-permute-done | bytes 2097184 | tf_op jit(solution)/shard_map/ppermute | solution.py:431
  389.0 14.9 %collective-permute-done.5 = bf16[1024,512]{1,0:T(8,128)(2,1)S(1)} collective-permute-done((bf16[1024,512]{1,0:T(8,128)(2,1)S(1)}, bf16[1024,512]{1,0:T(8,128)(2,1)S(1)}, u32[]{:S(2)}, u32[]{:S(2)}) %collective-permute-start.5) | collective-permute-done | bytes 1048608 | tf_op jit(solution)/shard_map/ppermute | solution.py:431
  405.3 48.4 %attend_back.1 = bf16[1024,3072]{1,0:T(8,128)(2,1)} custom-call(f32[16]{0:T(128)S(1)} %multiply_exponential_fusion.slope_ref, bf16[1024,3072]{1,0:T(8,128)(2,1)} %add_convert_fusion.packed_ref, bf16[1024,1024]{1,0:T(8,128)(2,1)S(1)} %convolution_convert_fusion.1.d_context_ref, f32[8,2,1024]{2,1,0:T(2,128)S(1)} %get-tuple-element.26.lse_ref), custom_call_target="tpu_custom_call" | custom-call | flops 42949672960 | bytes 14680064 | tf_op jit(solution)/shard_map/attend_back/pallas_call | solution.py:390
  471.2 20.6 %fusion.20 = (f32[1024]{0:T(1024)S(1)}, f32[1024]{0:T(1024)S(1)}, f32[1024]{0:T(1024)S(1)}, f32[1024]{0:T(1024)S(1)}, f32[1024,1024]{1,0:T(8,128)S(1)}) fusion(f32[1024]{0:T(1024)S(1)} %copy-done.47, f32[1024]{0:T(1024)S(1)} %copy-done.42, bf16[1024,512]{1,0:T(8,128)(2,1)S(1)} %copy-done.3, bf16[1024,512]{1,0:T(8,128)(2,1)S(1)} %copy-done.9, pred[]{:T(512)S(6)} %eq.11, ...), kind=kOutput, calls=%fused_computation.38 | convolution fusion | flops 6512701440 | bytes 18903040 | tf_op jit(solution)/shard_map/dot_general | solution.py:285
  491.9 5.9 add_convert_fusion.3
  499.8 34.8 %collective-permute-done.16 = bf16[512,1536]{1,0:T(8,128)(2,1)S(1)} collective-permute-done((bf16[512,1536]{1,0:T(8,128)(2,1)S(1)}, bf16[512,1536]{1,0:T(8,128)(2,1)S(1)}, u32[]{:S(2)}, u32[]{:S(2)}) %collective-permute-start.16) | collective-permute-done | bytes 1572896 | tf_op jit(solution)/shard_map/ppermute | solution.py:431
  542.6 12.4 %collective-permute-done.11 = f32[13312]{0:T(1024)S(1)} collective-permute-done((f32[13312]{0:T(1024)S(1)}, f32[13312]{0:T(1024)S(1)}, u32[]{:S(2)}, u32[]{:S(2)}) %collective-permute-start.11) | collective-permute-done | bytes 53280 | tf_op jit(solution)/shard_map/ppermute | solution.py:431
  557.4 10.3 %collective-permute-done.12 = f32[13312]{0:T(1024)S(1)} collective-permute-done((f32[13312]{0:T(1024)S(1)}, f32[13312]{0:T(1024)S(1)}, u32[]{:S(2)}, u32[]{:S(2)}) %collective-permute-start.12) | collective-permute-done | bytes 53280 | tf_op jit(solution)/shard_map/ppermute | solution.py:431
  595.2 26.9 %all-reduce.10.cloned.1.call-done = (bf16[512,768]{1,0:T(8,128)(2,1)}, bf16[256,512]{1,0:T(8,128)(2,1)}) async-done(((bf16[512,768]{1,0:T(8,128)(2,1)}, bf16[256,512]{1,0:T(8,128)(2,1)}), (bf16[512,768]{1,0:T(8,128)(2,1)}, bf16[256,512]{1,0:T(8,128)(2,1)})) %all-reduce.10.cloned.1.call-update) | async-done | bytes 1048592 | tf_op jit(solution)/shard_map/psum | solution.py:592
  (277 shorter events, 152.2 us)
Async XLA Ops:
  7.2 49.1 %all-gather.6.cloned.1.call-start = ((), (), s32[]{:S(2)}) async-start(), calls=%async_computation | async-start | bytes 2359296 | tf_op jit(solution)/shard_map/all_gather | solution.py:440
  7.9 97.8 %all-gather.12.cloned.1.call-start = ((), (), s32[]{:S(2)}) async-start(), calls=%async_computation.5 | async-start | bytes 7299072 | tf_op jit(solution)/shard_map/all_gather | solution.py:450
  17.0 156.9 %all-gather.8.cloned.1.call-start = ((), (), s32[]{:S(2)}) async-start(), calls=%async_computation.1 | async-start | bytes 9437184 | tf_op jit(solution)/shard_map/all_gather | solution.py:440
  17.7 200.5 %all-gather.10.cloned.1.call-start = ((), (), s32[]{:S(2)}) async-start(), calls=%async_computation.2 | async-start | bytes 9437184 | tf_op jit(solution)/shard_map/all_gather | solution.py:440
  18.3 438.8 %all-reduce.6.cloned.1.call-start = ((), (), s32[]{:S(2)}) async-start(), calls=%async_computation.3 | async-start | bytes 2097152 | tf_op jit(solution)/shard_map/psum | solution.py:581
  19.5 34.5 %collective-permute-start = (bf16[1024,512]{1,0:T(8,128)(2,1)}, bf16[1024,512]{1,0:T(8,128)(2,1)S(1)}, u32[]{:S(2)}, u32[]{:S(2)}) collective-permute-start(bf16[1024,512]{1,0:T(8,128)(2,1)} %get-tuple-element.81), channel_id=1, source_target_pairs={{0,1},{1,0},{2,3},{3,2},{4,5},{5,4},{6,7},{7,6},{8,9},{9,8},{10,11... | collective-permute-start | bytes 3145736 | tf_op jit(solution)/shard_map/ppermute | solution.py:431
  23.6 198.4 %collective-permute-start.2 = (bf16[1024,512]{1,0:T(8,128)(2,1)}, bf16[1024,512]{1,0:T(8,128)(2,1)}, u32[]{:S(2)}, u32[]{:S(2)}) collective-permute-start(bf16[1024,512]{1,0:T(8,128)(2,1)} %get-tuple-element.78), channel_id=1, source_target_pairs={{0,1},{1,0},{2,3},{3,2},{4,5},{5,4},{6,7},{7,6},{8,9},{9,8},{10,11... | collective-permute-start | bytes 3145736 | tf_op jit(solution)/shard_map/ppermute | solution.py:431
  263.8 36.5 %collective-permute-start.6 = (bf16[1024,2048]{1,0:T(8,128)(2,1)}, bf16[1024,2048]{1,0:T(8,128)(2,1)}, u32[]{:S(2)}, u32[]{:S(2)}) collective-permute-start(bf16[1024,2048]{1,0:T(8,128)(2,1)} %fusion.39), channel_id=1, source_target_pairs={{0,2},{2,0},{4,6},{6,4},{1,3},{3,1},{5,7},{7,5},{8,10},{10,8},{12,... | collective-permute-start | bytes 12582920 | tf_op jit(solution)/shard_map/ppermute | solution.py:431
  275.8 36.1 %collective-permute-start.3 = (bf16[2048,1024]{1,0:T(8,128)(2,1)}, bf16[2048,1024]{1,0:T(8,128)(2,1)}, u32[]{:S(2)}, u32[]{:S(2)}) collective-permute-start(bf16[2048,1024]{1,0:T(8,128)(2,1)} %fusion.42), channel_id=1, source_target_pairs={{0,2},{2,0},{4,6},{6,4},{1,3},{3,1},{5,7},{7,5},{8,10},{10,8},{12,... | collective-permute-start | bytes 12582920 | tf_op jit(solution)/shard_map/ppermute | solution.py:431
  300.1 77.2 %collective-permute-start.18 = (bf16[512,1024]{1,0:T(8,128)(2,1)}, bf16[512,1024]{1,0:T(8,128)(2,1)}, u32[]{:S(2)}, u32[]{:S(2)}) collective-permute-start(bf16[512,1024]{1,0:T(8,128)(2,1)} %convolution_convert_fusion.2), channel_id=1, source_target_pairs={{0,2},{2,0},{4,6},{6,4},{1,3},{3,1},{5,7},{7,5},{8,10},{10,8},{12,... | collective-permute-start | bytes 3145736 | tf_op jit(solution)/shard_map/ppermute | solution.py:431
  310.9 72.7 %collective-permute-start.7 = (bf16[512,2048]{1,0:T(8,128)(2,1)}, bf16[512,2048]{1,0:T(8,128)(2,1)}, u32[]{:S(2)}, u32[]{:S(2)}) collective-permute-start(bf16[512,2048]{1,0:T(8,128)(2,1)} %constant_dynamic-slice_fusion.14), channel_id=1, source_target_pairs={{0,1},{1,0},{2,3},{3,2},{4,5},{5,4},{6,7},{7,6},{8,9},{9,8},{10,11... | collective-permute-start | bytes 6291464 | tf_op jit(solution)/shard_map/ppermute | solution.py:431
  325.4 48.1 %collective-permute-start.4 = (bf16[1024,1024]{1,0:T(8,128)(2,1)}, bf16[1024,1024]{1,0:T(8,128)(2,1)}, u32[]{:S(2)}, u32[]{:S(2)}) collective-permute-start(bf16[1024,1024]{1,0:T(8,128)(2,1)} %constant_dynamic-slice_fusion.20), channel_id=1, source_target_pairs={{0,4},{2,6},{4,0},{6,2},{1,5},{3,7},{5,1},{7,3},{8,12},{10,14},{12... | collective-permute-start | bytes 6291464 | tf_op jit(solution)/shard_map/ppermute | solution.py:431
  343.7 38.3 %collective-permute-start.1 = (bf16[1024,512]{1,0:T(8,128)(2,1)S(1)}, bf16[1024,512]{1,0:T(8,128)(2,1)S(1)}, u32[]{:S(2)}, u32[]{:S(2)}) collective-permute-start(bf16[1024,512]{1,0:T(8,128)(2,1)S(1)} %dynamic-slice_convert_fusion.1), channel_id=1, source_target_pairs={{0,1},{1,0},{2,3},{3,2},{4,5},{5,4},{6,7},{7,6},{8,9},{9,8},{10,11... | collective-permute-start | bytes 3145736 | tf_op jit(solution)/shard_map/ppermute | solution.py:431
  376.2 27.7 %collective-permute-start.5 = (bf16[1024,512]{1,0:T(8,128)(2,1)S(1)}, bf16[1024,512]{1,0:T(8,128)(2,1)S(1)}, u32[]{:S(2)}, u32[]{:S(2)}) collective-permute-start(bf16[1024,512]{1,0:T(8,128)(2,1)S(1)} %constant_dynamic-slice_fusion.19), channel_id=1, source_target_pairs={{0,1},{1,0},{2,3},{3,2},{4,5},{5,4},{6,7},{7,6},{8,9},{9,8},{10,11... | collective-permute-start | bytes 3145736 | tf_op jit(solution)/shard_map/ppermute | solution.py:431
  380.8 86.9 %collective-permute-start.19 = (bf16[256,1024]{1,0:T(8,128)(2,1)}, bf16[256,1024]{1,0:T(8,128)(2,1)}, u32[]{:S(2)}, u32[]{:S(2)}) collective-permute-start(bf16[256,1024]{1,0:T(8,128)(2,1)} %constant_dynamic-slice_fusion.1), channel_id=1, source_target_pairs={{0,4},{2,6},{4,0},{6,2},{1,5},{3,7},{5,1},{7,3},{8,12},{10,14},{12... | collective-permute-start | bytes 1572872 | tf_op jit(solution)/shard_map/ppermute | solution.py:431
  387.4 66.3 %collective-permute-start.8 = (bf16[512,1024]{1,0:T(8,128)(2,1)S(1)}, bf16[512,1024]{1,0:T(8,128)(2,1)}, u32[]{:S(2)}, u32[]{:S(2)}) collective-permute-start(bf16[512,1024]{1,0:T(8,128)(2,1)S(1)} %constant_dynamic-slice_fusion.13), channel_id=1, source_target_pairs={{0,4},{2,6},{4,0},{6,2},{1,5},{3,7},{5,1},{7,3},{8,12},{10,14},{12... | collective-permute-start | bytes 3145736 | tf_op jit(solution)/shard_map/ppermute | solution.py:431
  405.2 165.0 %all-reduce.8.cloned.1.call-start = ((), (), s32[]{:S(2)}) async-start(), calls=%async_computation.4 | async-start | bytes 2097152 | tf_op jit(solution)/shard_map/psum | solution.py:584
  467.6 24.2 %collective-permute-start.15 = (bf16[1024,1536]{1,0:T(8,128)(2,1)}, bf16[1024,1536]{1,0:T(8,128)(2,1)}, u32[]{:S(2)}, u32[]{:S(2)}) collective-permute-start(bf16[1024,1536]{1,0:T(8,128)(2,1)} %convolution_convert_fusion), channel_id=1, source_target_pairs={{0,2},{2,0},{4,6},{6,4},{1,3},{3,1},{5,7},{7,5},{8,10},{10,8},{12,... | collective-permute-start | bytes 9437192 | tf_op jit(solution)/shard_map/ppermute | solution.py:431
  469.7 86.0 %collective-permute-start.20 = (bf16[256,512]{1,0:T(8,128)(2,1)}, bf16[256,512]{1,0:T(8,128)(2,1)}, u32[]{:S(2)}, u32[]{:S(2)}) collective-permute-start(bf16[256,512]{1,0:T(8,128)(2,1)} %constant_dynamic-slice_fusion), channel_id=1, source_target_pairs={{0,1},{1,0},{2,3},{3,2},{4,5},{5,4},{6,7},{7,6},{8,9},{9,8},{10,11... | collective-permute-start | bytes 786440 | tf_op jit(solution)/shard_map/ppermute | solution.py:431
  471.2 151.0 %all-reduce.10.cloned.1.call-start = ((), (), s32[]{:S(2)}) async-start(), calls=%async_computation.6 | async-start | bytes 2097152 | tf_op jit(solution)/shard_map/psum | solution.py:592
  498.0 36.6 %collective-permute-start.16 = (bf16[512,1536]{1,0:T(8,128)(2,1)S(1)}, bf16[512,1536]{1,0:T(8,128)(2,1)S(1)}, u32[]{:S(2)}, u32[]{:S(2)}) collective-permute-start(bf16[512,1536]{1,0:T(8,128)(2,1)S(1)} %constant_dynamic-slice_fusion.7), channel_id=1, source_target_pairs={{0,1},{1,0},{2,3},{3,2},{4,5},{5,4},{6,7},{7,6},{8,9},{9,8},{10,11... | collective-permute-start | bytes 4718600 | tf_op jit(solution)/shard_map/ppermute | solution.py:431
  499.7 39.2 %collective-permute-start.10 = (f32[13312]{0:T(1024)S(1)}, f32[13312]{0:T(1024)S(1)}, u32[]{:S(2)}, u32[]{:S(2)}) collective-permute-start(f32[13312]{0:T(1024)S(1)} %constant_dynamic-update-slice_fusion), channel_id=1, source_target_pairs={{0,2},{2,0},{4,6},{6,4},{1,3},{3,1},{5,7},{7,5},{8,10},{10,8},{12,... | collective-permute-start | bytes 159752 | tf_op jit(solution)/shard_map/ppermute | solution.py:431
  535.0 34.1 %collective-permute-start.17 = (bf16[512,768]{1,0:T(8,128)(2,1)S(1)}, bf16[512,768]{1,0:T(8,128)(2,1)S(1)}, u32[]{:S(2)}, u32[]{:S(2)}) collective-permute-start(bf16[512,768]{1,0:T(8,128)(2,1)S(1)} %constant_dynamic-slice_fusion.6), channel_id=1, source_target_pairs={{0,4},{2,6},{4,0},{6,2},{1,5},{3,7},{5,1},{7,3},{8,12},{10,14},{12... | collective-permute-start | bytes 2359304 | tf_op jit(solution)/shard_map/ppermute | solution.py:431
  542.1 47.1 %collective-permute-start.9 = (bf16[1024,512]{1,0:T(8,128)(2,1)}, bf16[1024,512]{1,0:T(8,128)(2,1)}, u32[]{:S(2)}, u32[]{:S(2)}) collective-permute-start(bf16[1024,512]{1,0:T(8,128)(2,1)} %dynamic-slice_convert_fusion), channel_id=1, source_target_pairs={{0,1},{1,0},{2,3},{3,2},{4,5},{5,4},{6,7},{7,6},{8,9},{9,8},{10,11... | collective-permute-start | bytes 3145736 | tf_op jit(solution)/shard_map/ppermute | solution.py:431
  (63 other events, 1045.3 us)
Sparse Core Ops, SparseCore 0:
  9.9 38.1 all-gather.5
  50.6 55.1 all-gather.11
  107.6 54.3 all-gather.7
  163.8 54.3 all-gather.9
  405.3 51.8 all-reduce.5
  471.3 51.0 all-reduce.7
  570.3 51.7 all-reduce.9
